TPU v7x, 512 devices: a whole 4x4x16 slice. The times are simulated.
512 devices in a mesh: dp: 64 (over z, y), head: 8 (over x, core).
Axes of the slice: x: 4, y: 4, z: 16, core: 2. Of those that a mesh axis runs over, the one named last changes fastest.
Arguments:
- tokens: bfloat16 [8192, 1536], P('dp'), may hold values from -6 to 6
- cotangent: bfloat16 [8192, 1536], P('dp'), may hold values from -2 to 2
- w_qkv: bfloat16 [1536, 3, 1024], P(None, None, 'head'), may hold values from -0.15625 to 0.15625
- w_out: bfloat16 [1024, 1536], P('head'), may hold values from -0.5 to 0.5
- qk_gain: float32 [2, 64], replicated, may hold values from 1 to 4.5
- modulation: bfloat16 [32, 3, 1536], replicated, may hold values from -4 to 4
- image_counts: int32 [32], replicated, may hold values from 1 to 768, as said below
Outputs:
- layer_out: bfloat16 [8192, 1536], P(('dp', 'head'))
- input_grad: bfloat16 [8192, 1536], P(('dp', 'head'))
Inputs may be any that keep to these rules, and one draw needn't show every extreme that they name: `image_counts`: the counts sum to 8192; each image's rows are consecutive in the pack, images in the order of this array; 8 of the images, at places drawn anew, hold exactly 768 tokens each, and every other image fewer.
All inputs are finite; a program needn't handle non-finite values.
Results may differ from a plain program's by a relative error of at most 0.028.
The roundings to bfloat16 on the way count: a program that leaves them out, or rounds other values in their place, can miss the bound.
Values may be sent and summed in bfloat16 or wider, within the bound.
No kernel may reach another device: no remote copies, remote signals or barrier semaphores. Data moves between devices by JAX's collectives and lax.ppermute only.
A program may use at most 64 MiB of HBM per device.

v0:
```python
import math

import jax
import jax.numpy as jnp
from jax import lax
from jax.experimental import pallas as pl
from jax.experimental.pallas import tpu as pltpu
from jax.sharding import PartitionSpec as P

EPS = 1e-06
SAME_IMAGE = 512.0
LANES = 128
HEAD = 64
F32 = jnp.float32
BF16 = jnp.bfloat16
VMEM_LIMIT = 24 * 1024 * 1024
ENTER_LIMIT = 60 * 1024 * 1024
VMEM = pl.BlockSpec(memory_space=pltpu.VMEM)
SMEM = pl.BlockSpec(memory_space=pltpu.SMEM)


def rows_dot(a, b):
    return lax.dot_general(a, b, (((1,), (1,)), ((), ())), preferred_element_type=F32)


def block_index():
    return (lax.axis_index("z") * 2 + lax.axis_index("yh")) * 2 + lax.axis_index("yl")


def image_bounds(counts_ref, first_lane):
    lane = lax.broadcasted_iota(jnp.int32, (1, LANES), 1)
    starts = jnp.zeros((1, LANES), jnp.int32)
    ends = jnp.zeros((1, LANES), jnp.int32)
    total = jnp.int32(0)
    for image in range(counts_ref.shape[0]):
        here = lane == first_lane + image
        starts = jnp.where(here, total, starts)
        total = total + counts_ref[image]
        ends = jnp.where(here, total, ends)
    return starts, ends


def modulation_rows(counts_ref, modulation_ref, first, rows):
    starts, ends = image_bounds(counts_ref, 0)
    place = first + lax.broadcasted_iota(jnp.int32, (rows, LANES), 0)
    member = ((place >= starts) & (place < ends)).astype(F32).astype(BF16)
    member = member[:, : modulation_ref.shape[1]]
    return [
        jnp.dot(member, modulation_ref[part], preferred_element_type=F32) for part in range(3)
    ]


def layer_norm(values):
    average = jnp.mean(values, axis=-1, keepdims=True)
    centred = values - average
    inv_std = lax.rsqrt(jnp.mean(centred * centred, axis=-1, keepdims=True) + EPS)
    return centred * inv_std, inv_std


def head_sums(values):
    lanes = (LANES, LANES)
    first = lax.broadcasted_iota(jnp.int32, lanes, 0) < HEAD
    second = lax.broadcasted_iota(jnp.int32, lanes, 1) < HEAD
    ones = (first == second).astype(F32).astype(BF16)
    large = values.astype(BF16)
    small = (values - large.astype(F32)).astype(BF16)
    large = jnp.dot(large, ones, preferred_element_type=F32)
    return large + jnp.dot(small, ones, preferred_element_type=F32)


def both_heads(gains_ref, which):
    gain = gains_ref[which : which + 1, :]
    return jnp.concatenate([gain, gain], axis=1)


def head_scale(raw):
    return lax.rsqrt(head_sums(raw * raw) * (1.0 / HEAD) + EPS)


def enter_kernel(
    counts_ref,
    gains_ref,
    tokens_ref,
    cotangent_ref,
    w_qkv_ref,
    w_out_ref,
    modulation_ref,
    out_ref,
    raw_ref,
    raw_far_ref,
    rows_ref,
):
    rows = tokens_ref.shape[0]
    first = block_index() * rows
    shift, scale, gate = modulation_rows(counts_ref, modulation_ref, first, rows)
    normed, _ = layer_norm(tokens_ref[...].astype(F32))
    hidden = (normed * (1.0 + scale) + shift).astype(BF16)
    weights = jnp.concatenate([w_qkv_ref[part] for part in range(3)], axis=1)
    qkv = jnp.dot(hidden, weights, preferred_element_type=F32)
    q, k, v = (qkv[:, part * LANES : (part + 1) * LANES] for part in range(3))
    d_mixed = (cotangent_ref[...].astype(F32) * gate).astype(BF16)
    d_attn = rows_dot(d_mixed, w_out_ref[...])
    rows_ref[0] = q.astype(BF16)
    rows_ref[1] = k.astype(BF16)
    q = rows_ref[0].astype(F32)
    k = rows_ref[1].astype(F32)
    q = q * head_scale(q) * (both_heads(gains_ref, 0) * (1.0 / math.sqrt(HEAD)))
    k = k * head_scale(k) * both_heads(gains_ref, 1)
    core = lax.axis_index("core")
    share = raw_ref.shape[1] // 4
    for ref, side in ((raw_ref, core), (raw_far_ref, 1 - core)):
        for part in range(4):
            begin = pl.multiple_of((2 * part + side) * share, share)
            for array in range(2):
                ref[array, part * share : (part + 1) * share, :] = rows_ref[
                    array, pl.ds(begin, share), :
                ]
    low = low_lanes()

    def beside(left, right):
        return jnp.where(low, left, right).astype(BF16)

    q_v = (beside(q, pltpu.roll(v, HEAD, 1)), beside(pltpu.roll(q, HEAD, 1), v))
    k_d = (beside(k, pltpu.roll(d_attn, HEAD, 1)), beside(pltpu.roll(k, HEAD, 1), d_attn))
    for place in range(out_ref.shape[0]):
        out_ref[place, :, 0:LANES] = q_v[place % 2]
        out_ref[place, :, LANES:] = k_d[place % 2]


def enter(counts, gains, tokens, cotangent, w_parts, w_out, modulation, quad):
    rows = tokens.shape[0]
    raw = jax.ShapeDtypeStruct((2, rows // 2, LANES), BF16)
    return pl.pallas_call(
        enter_kernel,
        out_shape=(jax.ShapeDtypeStruct((quad, rows, 2 * LANES), BF16), raw, raw),
        in_specs=[SMEM] + [VMEM] * 6,
        out_specs=(VMEM,) * 3,
        scratch_shapes=[pltpu.VMEM((2, rows, LANES), BF16)],
        compiler_params=pltpu.CompilerParams(vmem_limit_bytes=ENTER_LIMIT),
    )(counts, gains, tokens, cotangent, w_parts, w_out, modulation)


def pack_kernel(w_qkv_ref, w_out_ref, raw_ref, weights_ref, sems):
    width = w_out_ref.shape[1]
    rows = raw_ref.shape[1]
    pairs = []
    for part in range(3):
        pairs.append((w_qkv_ref.at[part], weights_ref.at[part * width : (part + 1) * width, :]))
    for tile in range(width // LANES):
        at = slice(tile * LANES, (tile + 1) * LANES)
        to = slice(3 * width + tile * LANES, 3 * width + (tile + 1) * LANES)
        pairs.append((w_out_ref.at[:, at], weights_ref.at[to, :]))
    for array in range(2):
        to = slice(4 * width + array * rows, 4 * width + (array + 1) * rows)
        pairs.append((raw_ref.at[array], weights_ref.at[to, :]))
    copies = [
        pltpu.make_async_copy(source, target, sems.at[place])
        for place, (source, target) in enumerate(pairs)
    ]
    for copy in copies:
        copy.start()
    for copy in copies:
        copy.wait()


def pack(w_parts, w_out, raw):
    width = w_out.shape[1]
    whole = pl.BlockSpec(memory_space=pl.ANY)
    return pl.pallas_call(
        pack_kernel,
        out_shape=jax.ShapeDtypeStruct((4 * width + 2 * raw.shape[1], LANES), BF16),
        in_specs=[whole] * 3,
        out_specs=VMEM,
        scratch_shapes=[pltpu.SemaphoreType.DMA((5 + width // LANES,))],
        compiler_params=pltpu.CompilerParams(vmem_limit_bytes=8 * 1024 * 1024),
    )(w_parts, w_out, raw)


def w_out_of(weights_ref, width):
    return jnp.concatenate(
        [
            weights_ref[3 * width + tile * LANES : 3 * width + (tile + 1) * LANES, :]
            for tile in range(width // LANES)
        ],
        axis=1,
    )


LOG2_E = math.log2(math.e)
INV_ROOT = 1.0 / math.sqrt(HEAD)
CHUNK = 256
TILE = 64
MAIN = 6
REACH_CHUNKS = 4


def low_lanes():
    return lax.broadcasted_iota(jnp.int32, (1, LANES), 1) < HEAD


def place_block(source, place, starts, ends, stores):
    low = low_lanes()
    rows = source.shape[0]
    at = place + lax.broadcasted_iota(jnp.int32, (rows, LANES), 0)
    same = ((at >= starts) & (at < ends)).astype(F32)
    first = source[:, 0:LANES].astype(F32)
    second = source[:, LANES:].astype(F32)
    q_store, k_store, v_store, d_store, kv_store = stores
    q_store[...] = jnp.where(low, first, same * SAME_IMAGE).astype(BF16)
    k_store[...] = jnp.where(low, second, same).astype(BF16)
    v_store[...] = jnp.where(low, 0.0, first).astype(BF16)
    d_store[...] = source[:, LANES:]
    kv_store[...] = jnp.where(low, second, first).astype(BF16).T


def window_facts(counts_ref):
    half = lax.axis_index("yh")
    origin = (block_index() // 4 - 1) * 2 * CHUNK
    own_at = (2 + half) * CHUNK
    starts, ends = image_bounds(counts_ref, HEAD)
    left_from = jnp.int32(-CHUNK)
    right_to = jnp.int32((MAIN + 1) * CHUNK)
    total = -origin
    for image in range(counts_ref.shape[0]):
        left_from = jnp.where(total <= own_at, total, left_from)
        ended = total >= own_at + CHUNK
        total = total + counts_ref[image]
        right_to = jnp.where((total >= own_at + CHUNK) & jnp.logical_not(ended), total, right_to)
    return half, own_at, starts - origin, ends - origin, left_from, right_to


def by_eight(values):
    return values.reshape(values.shape[0] // 8, 8, values.shape[1])


def add_tiles(s_ref, g_ref, rows, highest, total, grads):
    for piece in range(rows // TILE):
        at = slice(piece * TILE, (piece + 1) * TILE)
        weights = jnp.exp2(s_ref[at, :] * LOG2_E - highest)
        total = total + jnp.sum(by_eight(weights), axis=0)
        grads = grads + jnp.sum(by_eight(weights * g_ref[at, :]), axis=0)
    return total, grads


def rows_max(values):
    return jnp.max(by_eight(values), axis=0)


def chunks_from(key, count, *refs):
    rows = [pl.ds(pl.multiple_of(key + i * CHUNK, CHUNK), CHUNK) for i in range(count)]
    return [tuple(ref.at[at, :] for ref in refs) for at in rows]


def running_sums(pieces, q_block, d_block, s_ref, g_ref):
    highest = jnp.full((8, CHUNK), -jnp.inf, F32)
    total = jnp.zeros((8, CHUNK), F32)
    grads = jnp.zeros((8, CHUNK), F32)
    for piece, (keys_ref, values_ref) in enumerate(pieces):
        here = slice(piece * CHUNK, (piece + 1) * CHUNK)
        scores = rows_dot(keys_ref[...], q_block)
        s_ref[here, :] = scores
        g_ref[here, :] = rows_dot(values_ref[...], d_block)
        higher = jnp.maximum(highest, rows_max(scores) * LOG2_E)
        shrink = jnp.exp2(highest - higher)
        total = total * shrink
        grads = grads * shrink
        highest = higher
        for tile in range(CHUNK // TILE):
            at = slice(piece * CHUNK + tile * TILE, piece * CHUNK + (tile + 1) * TILE)
            weights = jnp.exp2(by_eight(s_ref[at, :]) * LOG2_E - highest[None])
            total = total + jnp.sum(weights, axis=0)
            grads = grads + jnp.sum(weights * by_eight(g_ref[at, :]), axis=0)
    top = jnp.max(highest, axis=0, keepdims=True)
    shrink = jnp.exp2(highest - top)
    total = jnp.sum(total * shrink, axis=0, keepdims=True)
    return top, total, jnp.sum(grads * shrink, axis=0, keepdims=True)


def near_kernel(
    counts_ref,
    first_ref,
    quad_ref,
    second_ref,
    qx_ref,
    kx_ref,
    vx_ref,
    dx_ref,
    kv_ref,
    so_ref,
    go_ref,
    sn_ref,
    gn_ref,
    stats_ref,
    s_ref,
    g_ref,
):
    half, own_at, starts, ends, left_from, right_to = window_facts(counts_ref)
    block_rows = CHUNK // 2

    def place(source, begin):
        begin = pl.multiple_of(begin, block_rows)
        at = pl.ds(begin, block_rows)
        stores = [ref.at[at, :] for ref in (qx_ref, kx_ref, vx_ref, dx_ref)]
        place_block(source, begin, starts, ends, stores + [kv_ref.at[:, at]])

    to_first = jnp.where(lax.rem(lax.axis_index("z"), 2) == 0, 2 * CHUNK, -2 * CHUNK)
    for block in range(4):
        at = slice(block * block_rows, (block + 1) * block_rows)
        begin = 2 * CHUNK + block * block_rows
        place(quad_ref.at[at], begin)
        place(first_ref.at[at], begin + to_first)
        place(second_ref.at[at], begin - to_first)

    own_rows = pl.ds(pl.multiple_of(own_at, CHUNK), CHUNK)
    q_own = qx_ref[own_rows, :]
    d_own = dx_ref[own_rows, :]
    highest = jnp.full((8, CHUNK), -jnp.inf, F32)
    for piece in range(MAIN):
        at = slice(piece * CHUNK, (piece + 1) * CHUNK)
        scores = rows_dot(kx_ref[at, :], q_own)
        so_ref[at, :] = scores
        highest = jnp.maximum(highest, rows_max(scores))
        go_ref[at, :] = rows_dot(vx_ref[at, :], d_own)
    highest = jnp.max(highest, axis=0, keepdims=True) * LOG2_E
    total = jnp.zeros((8, CHUNK), F32)
    grads = jnp.zeros((8, CHUNK), F32)
    for piece in range(MAIN * CHUNK // TILE):
        at = slice(piece * TILE, (piece + 1) * TILE)
        weights = jnp.exp2(so_ref[at, :] * LOG2_E - highest)
        so_ref[at, :] = weights
        total = total + jnp.sum(by_eight(weights), axis=0)
        grads = grads + jnp.sum(by_eight(weights * go_ref[at, :]), axis=0)
    stats_ref[MAIN, 0:1, :] = highest
    stats_ref[MAIN, 1:2, :] = jnp.sum(total, axis=0, keepdims=True)
    stats_ref[MAIN, 2:3, :] = jnp.sum(grads, axis=0, keepdims=True)

    left_key = jnp.clip((left_from + CHUNK) // CHUNK - 1, 0, MAIN - REACH_CHUNKS)
    right_key = jnp.clip((right_to - 1) // CHUNK - (REACH_CHUNKS - 1), 0, MAIN - REACH_CHUNKS)

    def one_chunk(step, carry):
        slot = step + jnp.where(step >= 2 + half, 1, 0)
        begin = slot * CHUNK

        @pl.when((begin < right_to) & (begin + CHUNK > left_from))
        def _():
            at = pl.ds(pl.multiple_of(begin, CHUNK), CHUNK)
            key = jnp.where(begin < own_at, left_key, right_key) * CHUNK
            q_block = qx_ref[at, :]
            d_block = dx_ref[at, :]
            pieces = chunks_from(key, REACH_CHUNKS, kx_ref, vx_ref)
            highest, total, grads = running_sums(pieces, q_block, d_block, s_ref, g_ref)
            stats_ref[slot, 0:1, :] = highest
            stats_ref[slot, 1:2, :] = total
            stats_ref[slot, 2:3, :] = grads
            near_at = pl.ds(pl.multiple_of(own_at - key, CHUNK), CHUNK)
            sn_ref[slot, :, :] = s_ref[near_at, :]
            gn_ref[slot, :, :] = g_ref[near_at, :]

        return carry

    lax.fori_loop(0, MAIN - 1, one_chunk, 0)


def attend_near(counts, first, quad, second):
    rows = MAIN * CHUNK
    head_rows = jax.ShapeDtypeStruct((rows, LANES), BF16)
    scores = jax.ShapeDtypeStruct((rows, CHUNK), F32)
    tiles = jax.ShapeDtypeStruct((MAIN, CHUNK, CHUNK), F32)
    return pl.pallas_call(
        near_kernel,
        out_shape=(head_rows,) * 4
        + (jax.ShapeDtypeStruct((LANES, rows), BF16),)
        + (scores, scores, tiles, tiles, jax.ShapeDtypeStruct((MAIN + 1, 8, CHUNK), F32)),
        in_specs=[SMEM] + [VMEM] * 3,
        out_specs=(VMEM,) * 10,
        scratch_shapes=[pltpu.VMEM((REACH_CHUNKS * CHUNK, CHUNK), F32)] * 2,
        cost_estimate=pl.CostEstimate(
            flops=9000000000, bytes_accessed=1 << 20, transcendentals=1 << 20
        ),
        compiler_params=pltpu.CompilerParams(vmem_limit_bytes=VMEM_LIMIT),
    )(counts, first, quad, second)


def far_kernel(
    counts_ref,
    far_ref,
    qx_ref,
    kx_ref,
    vx_ref,
    dx_ref,
    kv_ref,
    so_ref,
    go_ref,
    sn_ref,
    gn_ref,
    stats_ref,
    out_ref,
    qf_ref,
    kf_ref,
    vf_ref,
    df_ref,
    kvf_ref,
    s_ref,
    g_ref,
    p_ref,
    d_ref,
    pn_ref,
    dn_ref,
    sums_ref,
    dk_ref,
    dv_ref,
    own_out_ref,
    done_ref,
):
    half, own_at, starts, ends, left_from, right_to = window_facts(counts_ref)
    block_rows = CHUNK // 2
    rows = MAIN * CHUNK
    far_at = jnp.where(half == 0, -CHUNK, rows)
    for block in range(2):
        at = slice(block * block_rows, (block + 1) * block_rows)
        stores = [ref.at[at, :] for ref in (qf_ref, kf_ref, vf_ref, df_ref)]
        place_block(
            far_ref.at[at],
            far_at + block * block_rows,
            starts,
            ends,
            stores + [kvf_ref.at[:, at]],
        )

    own_rows = pl.ds(pl.multiple_of(own_at, CHUNK), CHUNK)
    q_own = qx_ref[own_rows, :]
    d_own = dx_ref[own_rows, :]
    scores = rows_dot(kf_ref[...], q_own)
    s_ref[0:CHUNK, :] = scores
    g_ref[0:CHUNK, :] = rows_dot(vf_ref[...], d_own)
    near_highest = stats_ref[MAIN, 0:1, :]
    highest = jnp.max(rows_max(scores), axis=0, keepdims=True) * LOG2_E
    highest = jnp.maximum(near_highest, highest)
    shrink = jnp.exp2(near_highest - highest)
    zeros = jnp.zeros((8, CHUNK), F32)
    total, grads = add_tiles(s_ref, g_ref, CHUNK, highest, zeros, zeros)
    total = jnp.sum(total, axis=0, keepdims=True) + stats_ref[MAIN, 1:2, :] * shrink
    grads = jnp.sum(grads, axis=0, keepdims=True) + stats_ref[MAIN, 2:3, :] * shrink
    scale = 1.0 / total
    mean_grad = grads * scale

    near_scale = shrink * scale
    for piece in range(rows // TILE):
        at = slice(piece * TILE, (piece + 1) * TILE)
        probs = so_ref[at, :] * near_scale
        p_ref[at, :] = probs.astype(BF16)
        d_ref[at, :] = (probs * (go_ref[at, :] - mean_grad)).astype(BF16)
    for piece in range(CHUNK // TILE):
        at = slice(piece * TILE, (piece + 1) * TILE)
        to = slice(rows + piece * TILE, rows + (piece + 1) * TILE)
        probs = jnp.exp2(s_ref[at, :] * LOG2_E - highest) * scale
        p_ref[to, :] = probs.astype(BF16)
        d_ref[to, :] = (probs * (g_ref[at, :] - mean_grad)).astype(BF16)
    pn_ref[:, own_rows] = p_ref[own_rows, :]
    dn_ref[:, own_rows] = d_ref[own_rows, :]

    def times_window(values_ref):
        main = jnp.dot(kv_ref[...], values_ref[0:rows, :], preferred_element_type=F32)
        return main + jnp.dot(
            kvf_ref[...], values_ref[rows : rows + CHUNK, :], preferred_element_type=F32
        )

    upper = lax.broadcasted_iota(jnp.int32, (LANES, CHUNK), 0) < HEAD
    own_out_ref[...] = jnp.where(
        upper, times_window(d_ref) * INV_ROOT, times_window(p_ref)
    ).T

    query_lane = lax.broadcasted_iota(jnp.int32, (1, CHUNK), 1)
    reaches_far = jnp.where(half == 0, left_from < 0, right_to > rows)
    sums_ref[...] = stats_ref[...]
    dk_ref[...] = jnp.zeros_like(dk_ref)
    dv_ref[...] = jnp.zeros_like(dv_ref)

    @pl.when(reaches_far)
    def _():
        for step in range(2):
            slot = half * (MAIN - 2) + step
            at = pl.ds(pl.multiple_of(slot * CHUNK, CHUNK), CHUNK)
            space = pl.ds((REACH_CHUNKS + step) * CHUNK, CHUNK)
            highest, total, grads = running_sums(
                [(kf_ref, vf_ref)], qx_ref[at, :], dx_ref[at, :], s_ref.at[space], g_ref.at[space]
            )
            before = sums_ref[slot, 0:1, :]
            higher = jnp.maximum(before, highest)
            old = jnp.exp2(before - higher)
            new = jnp.exp2(highest - higher)
            sums_ref[slot, 0:1, :] = higher
            sums_ref[slot, 1:2, :] = sums_ref[slot, 1:2, :] * old + total * new
            sums_ref[slot, 2:3, :] = sums_ref[slot, 2:3, :] * old + grads * new

        q_block = qf_ref[...]
        d_block = df_ref[...]
        key = half * (MAIN // 2) * CHUNK
        pieces = chunks_from(key, REACH_CHUNKS - 1, kx_ref, vx_ref) + [(kf_ref, vf_ref)]
        highest, total, grads = running_sums(pieces, q_block, d_block, s_ref, g_ref)
        place = query_lane + far_at
        scale = jnp.where((place >= left_from) & (place < right_to), 1.0 / total, 0.0)
        mean_grad = grads * scale
        for piece in range(CHUNK // TILE):
            at = slice(piece * TILE, (piece + 1) * TILE)
            near_at = pl.ds(pl.multiple_of(own_at - key + piece * TILE, TILE), TILE)
            probs = jnp.exp2(s_ref[near_at, :] * LOG2_E - highest) * scale
            p_ref[at, :] = probs.astype(BF16)
            d_ref[at, :] = (probs * (g_ref[near_at, :] - mean_grad)).astype(BF16)
        dk_ref[...] = jnp.dot(d_ref[0:CHUNK, :], q_block, preferred_element_type=F32)
        dv_ref[...] = jnp.dot(p_ref[0:CHUNK, :], d_block, preferred_element_type=F32)

    for step in range(MAIN - 1):
        slot = step + jnp.where(step >= 2 + half, 1, 0)
        begin = slot * CHUNK
        chunk_at = pl.ds(pl.multiple_of(begin, CHUNK), CHUNK)
        place = query_lane + begin
        valid = (place >= left_from) & (place < right_to)
        highest = sums_ref[slot, 0:1, :]
        scale = 1.0 / sums_ref[slot, 1:2, :]
        mean_grad = sums_ref[slot, 2:3, :] * scale
        for piece in range(CHUNK // TILE):
            at = slice(piece * TILE, (piece + 1) * TILE)
            probs = jnp.exp2(sn_ref[slot, at, :] * LOG2_E - highest) * scale
            d_scores = probs * (gn_ref[slot, at, :] - mean_grad)
            pn_ref[at, chunk_at] = jnp.where(valid, probs, 0.0).astype(BF16)
            dn_ref[at, chunk_at] = jnp.where(valid, d_scores, 0.0).astype(BF16)
    d_key = dk_ref[...] + jnp.dot(dn_ref[...], qx_ref[...], preferred_element_type=F32)
    d_value = dv_ref[...] + jnp.dot(pn_ref[...], dx_ref[...], preferred_element_type=F32)
    done_ref[:, 0:LANES] = own_out_ref[...].astype(BF16)
    done_ref[:, LANES:] = jnp.where(low_lanes(), d_key, d_value).astype(BF16)
    share = 16
    for member in range(out_ref.shape[0]):
        block, core = member // 2, member % 2
        for part in range(out_ref.shape[1] // share):
            begin = (block * 8 + part * 2 + core) * share
            out_ref[member, part * share : (part + 1) * share, :] = done_ref[
                begin : begin + share, :
            ]


def attend_far(counts, far, near_parts):
    return pl.pallas_call(
        far_kernel,
        out_shape=jax.ShapeDtypeStruct((4, CHUNK // 4, 2 * LANES), BF16),
        in_specs=[SMEM] + [VMEM] * (1 + len(near_parts)),
        out_specs=VMEM,
        scratch_shapes=[pltpu.VMEM((CHUNK, LANES), BF16)] * 4
        + [pltpu.VMEM((LANES, CHUNK), BF16)]
        + [pltpu.VMEM(((REACH_CHUNKS + 2) * CHUNK, CHUNK), F32)] * 2
        + [pltpu.VMEM(((MAIN + 1) * CHUNK, CHUNK), BF16)] * 2
        + [pltpu.VMEM((CHUNK, MAIN * CHUNK), BF16)] * 2
        + [pltpu.VMEM((MAIN + 1, 8, CHUNK), F32)]
        + [pltpu.VMEM((CHUNK, LANES), F32)] * 3
        + [pltpu.VMEM((CHUNK, 2 * LANES), BF16)],
        cost_estimate=pl.CostEstimate(
            flops=9000000000, bytes_accessed=1 << 20, transcendentals=1 << 20
        ),
        compiler_params=pltpu.CompilerParams(vmem_limit_bytes=VMEM_LIMIT),
    )(counts, far, *near_parts)


def project_kernel(parts_ref, gains_ref, raw_ref, weights_ref, weights_far_ref, out_ref):
    rows = parts_ref.shape[1]
    width = out_ref.shape[2] // 2
    share = out_ref.shape[1]
    core = lax.axis_index("core")
    low = low_lanes()
    q_gain = both_heads(gains_ref, 0)
    k_gain = both_heads(gains_ref, 1)

    def norm_grad(raw, gain, d_norm):
        raw = raw.astype(F32)
        inverse = head_scale(raw)
        scaled = d_norm * gain
        inner = head_sums(raw * scaled) * (1.0 / HEAD)
        return inverse * scaled - raw * (inverse * inverse * inverse * inner)

    def by_column(which, raw):
        head0 = parts_ref[which].astype(F32)
        head1 = parts_ref[2 + which].astype(F32)
        a0, a1 = head0[:, :LANES], head1[:, :LANES]
        b0, b1 = head0[:, LANES:], head1[:, LANES:]
        d_q = norm_grad(raw[0], q_gain, jnp.where(low, a0, pltpu.roll(a1, HEAD, 1)))
        attn = jnp.where(low, pltpu.roll(a0, HEAD, 1), a1).astype(BF16)
        d_k = norm_grad(raw[1], k_gain, jnp.where(low, b0, pltpu.roll(b1, HEAD, 1)))
        d_v = jnp.where(low, pltpu.roll(b0, HEAD, 1), b1)
        return attn, [values.astype(BF16) for values in (d_q, d_k, d_v)]

    raw_far = [
        weights_far_ref[4 * width + array * rows : 4 * width + (array + 1) * rows, :]
        for array in range(2)
    ]
    attn, grads = by_column(core, [raw_ref[0], raw_ref[1]])
    attn_far, grads_far = by_column(1 - core, raw_far)
    both = (weights_ref, weights_far_ref)
    mixed = jnp.dot(
        jnp.concatenate([attn, attn_far], axis=1),
        jnp.concatenate([w_out_of(ref, width) for ref in both], axis=0),
        preferred_element_type=F32,
    ).astype(BF16)
    weights = [ref[part * width : (part + 1) * width, :] for ref in both for part in range(3)]
    d_hidden = rows_dot(
        jnp.concatenate(grads + grads_far, axis=1), jnp.concatenate(weights, axis=1)
    ).astype(BF16)
    for place in range(out_ref.shape[0]):
        at = slice(place * share, (place + 1) * share)
        out_ref[place, :, :width] = mixed[at]
        out_ref[place, :, width:] = d_hidden[at]


def project(parts, gains, raw, weights, weights_far, x_count, width):
    return pl.pallas_call(
        project_kernel,
        out_shape=jax.ShapeDtypeStruct((x_count, parts.shape[1] // x_count, 2 * width), BF16),
        in_specs=[VMEM] * 5,
        out_specs=VMEM,
        compiler_params=pltpu.CompilerParams(vmem_limit_bytes=VMEM_LIMIT),
    )(parts, gains, raw, weights, weights_far)


def ready_kernel(
    counts_ref,
    tokens_ref,
    cotangent_ref,
    modulation_ref,
    rows_ref,
    factors_ref,
):
    rows = rows_ref.shape[1]
    first_row = (lax.axis_index("x") * 2 + lax.axis_index("core")) * rows
    first = block_index() * tokens_ref.shape[0] + first_row
    _, scale, gate = modulation_rows(counts_ref, modulation_ref, first, rows)
    at = pl.ds(pl.multiple_of(first_row, rows), rows)
    normed, inv_std = layer_norm(tokens_ref[at, :].astype(F32))
    rows_ref[0] = tokens_ref[at, :]
    rows_ref[1] = cotangent_ref[at, :]
    factors_ref[0] = gate
    factors_ref[1] = 1.0 + scale
    factors_ref[2] = normed
    factors_ref[3] = jnp.broadcast_to(inv_std, normed.shape)


def ready(counts, tokens, cotangent, modulation, share):
    width = tokens.shape[1]
    return pl.pallas_call(
        ready_kernel,
        out_shape=(
            jax.ShapeDtypeStruct((2, share, width), BF16),
            jax.ShapeDtypeStruct((4, share, width), F32),
        ),
        in_specs=[SMEM] + [VMEM] * 3,
        out_specs=(VMEM, VMEM),
        compiler_params=pltpu.CompilerParams(vmem_limit_bytes=VMEM_LIMIT),
    )(counts, tokens, cotangent, modulation)


def leave_kernel(rows_ref, factors_ref, shares_ref, layer_ref, grad_ref):
    width = layer_ref.shape[1]
    sums = shares_ref[0].astype(F32)
    for share in range(1, shares_ref.shape[0]):
        sums = sums + shares_ref[share].astype(F32)
    layer = rows_ref[0].astype(F32) + factors_ref[0] * sums[:, :width]
    layer_ref[...] = layer.astype(BF16)
    d_normed = sums[:, width:] * factors_ref[1]
    normed = factors_ref[2]
    input_grad = rows_ref[1].astype(F32) + factors_ref[3] * (
        d_normed
        - jnp.mean(d_normed, axis=-1, keepdims=True)
        - normed * jnp.mean(d_normed * normed, axis=-1, keepdims=True)
    )
    grad_ref[...] = input_grad.astype(BF16)


def leave(rows, factors, shares):
    out = jax.ShapeDtypeStruct(rows.shape[1:], BF16)
    return pl.pallas_call(
        leave_kernel,
        out_shape=(out, out),
        in_specs=[VMEM] * 3,
        out_specs=(VMEM, VMEM),
        compiler_params=pltpu.CompilerParams(vmem_limit_bytes=VMEM_LIMIT),
    )(rows, factors, shares)


def per_device(tokens, cotangent, w_qkv, w_out, qk_gain, modulation, image_counts):
    tok_rows, model_width = tokens.shape
    z_count = lax.axis_size("z")
    x_count = lax.axis_size("x")
    quad = 4
    pair_rows = 2 * tok_rows
    share = tok_rows // (2 * x_count)
    w_parts = w_qkv.transpose(1, 0, 2)
    mod_parts = modulation.transpose(1, 0, 2)

    heads, raw, raw_far = enter(
        image_counts, qk_gain, tokens, cotangent, w_parts, w_out, mod_parts, quad
    )
    _, tokens_late, cotangent_late, mod_late, w_parts_late, w_out_late = (
        lax.optimization_barrier((heads, tokens, cotangent, mod_parts, w_parts, w_out))
    )
    rows, factors = ready(image_counts, tokens_late, cotangent_late, mod_late, share)
    weights = pack(w_parts_late, w_out_late, raw_far)
    mine = lax.all_to_all(heads, ("yh", "yl"), 0, 0)
    mine, rows, factors, weights = lax.optimization_barrier((mine, rows, factors, weights))
    mine = mine.reshape(quad * tok_rows, 2 * LANES)
    evens = range(0, z_count, 2)
    swaps = [(i, i + 1) for i in evens], [((i - 1) % z_count, i) for i in evens]
    first, second = (
        lax.ppermute(mine, "z", pairs + [(j, i) for i, j in pairs]) for pairs in swaps
    )
    halves = 4 * z_count
    far_half = jnp.where(
        lax.axis_index("yh") == lax.axis_index("core"), mine[pair_rows:], mine[:pair_rows]
    )

    def far_source(target):
        z, yh, core = target // 4, target // 2 % 2, target % 2
        return (z + (2 if yh else -2)) % z_count * 4 + (yh ^ core) * 2 + core

    far = lax.ppermute(
        far_half, ("z", "yh", "core"), [(far_source(i), i) for i in range(halves)]
    )
    near_parts = attend_near(image_counts, first, mine, second)
    weights_far = lax.ppermute(weights, "core", [(0, 1), (1, 0)])
    parts = attend_far(image_counts, far, near_parts)
    parts = lax.all_to_all(parts, ("yl", "core"), 0, 0)
    partial = project(parts, qk_gain, raw, weights, weights_far, x_count, model_width)
    shares = lax.all_to_all(partial, "x", 0, 0)
    return leave(rows, factors, shares)


def solution(mesh):
    split = jax.sharding.Mesh(mesh.devices.reshape(16, 2, 2, 4, 2), ("z", "yh", "yl", "x", "core"))
    dp, head = ("z", "yh", "yl"), ("x", "core")
    in_specs = (P(dp, None), P(dp, None), P(None, None, head), P(head, None), P(), P(), P())
    out_specs = (P(dp + head, None), P(dp + head, None))
    return jax.shard_map(
        per_device, mesh=split, in_specs=in_specs, out_specs=out_specs, check_vma=False
    )
```

profile of v0, /device:TPU:16, one launch (start us, length us, event | category | flops | bytes accessed | tf_op | source)
XLA Modules:
  0.0 61.9 jit_solution(7278812582504460068)
XLA Ops:
  0.6 0.0 copy-start.2
  0.6 0.0 copy-start.3
  0.7 0.0 copy-start.4
  0.7 0.0 copy-start.10
  0.7 0.0 copy-start
  0.7 0.0 copy-start.1
  0.7 3.6 %shard_map.86 = (bf16[4,128,256]{2,1,0:T(8,128)(2,1)}, bf16[2,64,128]{2,1,0:T(8,128)(2,1)}, bf16[2,64,128]{2,1,0:T(8,128)(2,1)}) custom-call(s32[32]{0:T(128)} %counts_ref.7, f32[2,64]{1,0:T(2,128)} %gains_ref.3, bf16[128,1536]{1,0:T(8,128)(2,1)} %tokens_ref.2, bf16[128,1536]{1,0:T(8,128)(2,1)} %cotangent_ref.2, bf16[3,1536,128]{2,1,0:T(8,128)(2,1)} %bitcast.4, ...), custom_call_target="tpu_custom_call" | custom-call | tf_op jit(solution)/shard_map/pallas_call | solution.py:133
  4.3 9.1 %all-to-all-start = ((bf16[4,128,256]{2,1,0:T(8,128)(2,1)}), bf16[4,128,256]{2,1,0:T(8,128)(2,1)S(1)}, u32[]{:S(2)}, u32[]{:S(2)}) async-start(bf16[4,128,256]{2,1,0:T(8,128)(2,1)} %get-tuple-element.26), calls=%async_computation | async-start | bytes 524288 | tf_op jit(solution)/shard_map/all_to_all | solution.py:704
  13.4 0.0 copy-done.2
  13.4 0.0 copy-done.3
  13.4 0.0 copy-done.4
  13.4 0.0 copy-done.10
  13.4 0.8 %shard_map.87 = (bf16[2,16,1536]{2,1,0:T(8,128)(2,1)S(1)}, f32[4,16,1536]{2,1,0:T(8,128)S(1)}) custom-call(s32[32]{0:T(128)S(1)} %copy-done.10, bf16[128,1536]{1,0:T(8,128)(2,1)S(1)} %copy-done.2, bf16[128,1536]{1,0:T(8,128)(2,1)S(1)} %copy-done.3, bf16[3,32,1536]{2,1,0:T(8,128)(2,1)S(1)} %bitcast.7), custom_call_target="tpu_custom_call" | custom-call | tf_op jit(solution)/shard_map/pallas_call | solution.py:646
  14.2 0.0 copy-start.5
  14.2 0.7 %copy-done.5 = f32[4,16,1536]{2,1,0:T(8,128)} copy-done((f32[4,16,1536]{2,1,0:T(8,128)}, f32[4,16,1536]{2,1,0:T(8,128)S(1)}, u32[]{:S(2)}) %copy-start.5) | copy-done | bytes 393240
  15.0 0.0 copy-done
  15.0 0.0 copy-done.1
  15.0 0.0 copy-start.8
  15.0 0.8 %copy-done.8 = bf16[2,64,128]{2,1,0:T(8,128)(2,1)S(1)} copy-done((bf16[2,64,128]{2,1,0:T(8,128)(2,1)S(1)}, bf16[2,64,128]{2,1,0:T(8,128)(2,1)}, u32[]{:S(2)}) %copy-start.8) | copy-done | bytes 32792
  15.7 0.9 %shard_map.88.weights_ref = bf16[6272,128]{1,0:T(8,128)(2,1)S(1)} custom-call(bf16[3,1536,128]{2,1,0:T(8,128)(2,1)S(1)} %bitcast.5, bf16[128,1536]{1,0:T(8,128)(2,1)S(1)} %copy-done.1, bf16[2,64,128]{2,1,0:T(8,128)(2,1)S(1)} %copy-done.8), custom_call_target="tpu_custom_call" | custom-call | tf_op jit(solution)/shard_map/pallas_call | solution.py:169
  16.6 0.5 all-to-all-done
  17.1 1.9 %collective-permute-start.1 = (bf16[512,256]{1,0:T(8,128)(2,1)S(1)}, bf16[512,256]{1,0:T(8,128)(2,1)S(1)}, u32[]{:S(2)}, u32[]{:S(2)}) collective-permute-start(bf16[512,256]{1,0:T(8,128)(2,1)S(1)} %bitcast.8), channel_id=1, source_target_pairs={{0,32},{64,96},{128,160},{192,224},{256,288},{320,352},{384,416},{... | collective-permute-start | bytes 786440 | tf_op jit(solution)/shard_map/ppermute | solution.py:710
  19.1 8.1 %collective-permute-start.2 = (bf16[512,256]{1,0:T(8,128)(2,1)S(1)}, bf16[512,256]{1,0:T(8,128)(2,1)S(1)}, u32[]{:S(2)}, u32[]{:S(2)}) collective-permute-start(bf16[512,256]{1,0:T(8,128)(2,1)S(1)} %bitcast.9), channel_id=1, source_target_pairs={{480,0},{32,64},{96,128},{160,192},{224,256},{288,320},{352,384},{... | collective-permute-start | bytes 786440 | tf_op jit(solution)/shard_map/ppermute | solution.py:710
  27.2 3.3 %collective-permute-start = (bf16[256,256]{1,0:T(8,128)(2,1)S(1)}, bf16[256,256]{1,0:T(8,128)(2,1)S(1)}, u32[]{:S(2)}, u32[]{:S(2)}) collective-permute-start(bf16[256,256]{1,0:T(8,128)(2,1)S(1)} %bitcast.11), channel_id=1, source_target_pairs={{448,0},{465,1},{80,16},{65,17},{480,32},{497,33},{112,48},{97,49}... | collective-permute-start | bytes 393224 | tf_op jit(solution)/shard_map/ppermute | solution.py:721
  30.6 1.9 %collective-permute-start.3 = (bf16[6272,128]{1,0:T(8,128)(2,1)S(1)}, bf16[6272,128]{1,0:T(8,128)(2,1)S(1)}, u32[]{:S(2)}, u32[]{:S(2)}) collective-permute-start(bf16[6272,128]{1,0:T(8,128)(2,1)S(1)} %shard_map.88.weights_ref), channel_id=1, source_target_pairs={{0,1},{1,0},{2,3},{3,2},{4,5},{5,4},{6,7},{7,6},{8,9},{9,8},{10,11... | collective-permute-start | bytes 4816904 | tf_op jit(solution)/shard_map/ppermute | solution.py:725
  32.5 0.0 collective-permute-done.1.first_ref
  32.5 1.0 %collective-permute-done.2.second_ref = bf16[512,256]{1,0:T(8,128)(2,1)S(1)} collective-permute-done((bf16[512,256]{1,0:T(8,128)(2,1)S(1)}, bf16[512,256]{1,0:T(8,128)(2,1)S(1)}, u32[]{:S(2)}, u32[]{:S(2)}) %collective-permute-start.2) | collective-permute-done | bytes 262176 | tf_op jit(solution)/shard_map/ppermute | solution.py:710
  33.5 3.7 %shard_map.89 = (bf16[1536,128]{1,0:T(8,128)(2,1)S(1)}, bf16[1536,128]{1,0:T(8,128)(2,1)S(1)}, bf16[1536,128]{1,0:T(8,128)(2,1)S(1)}, bf16[1536,128]{1,0:T(8,128...) custom-call(s32[32]{0:T(128)S(1)} %copy-done.10, ...), custom_call_target="tpu_custom_call" | custom-call | flops 8999999488 | bytes 1048576 | tf_op jit(solution)/shard_map/pallas_call | solution.py:369
  37.2 0.0 collective-permute-done.far_ref
  37.2 0.0 copy-start.7
  37.2 0.0 copy-start.9
  37.2 3.5 %shard_map.90 = bf16[4,64,256]{2,1,0:T(8,128)(2,1)S(1)} custom-call(s32[32]{0:T(128)S(1)} %copy-done.10, bf16[256,256]{1,0:T(8,128)(2,1)S(1)} %collective-permute-done.far_ref, bf16[1536,128]{1,0:T(8,128)(2,1)S(1)} %get-tuple-element.38.qx_ref, bf16[1536,128]{1,0:T(8,128)(2,1)S(1)} %get-tuple-element.39.kx_ref, ...), custom_call_target="tpu_custom_call" | custom-call | flops 8999999488 | bytes 1048576 | tf_op jit(solution)/shard_map/pallas_call | solution.py:543
  40.7 7.4 %all_to_all.15.parts_ref = bf16[4,64,256]{2,1,0:T(8,128)(2,1)S(1)} all-to-all(bf16[4,64,256]{2,1,0:T(8,128)(2,1)S(1)} %shard_map.90), channel_id=1, replica_groups=mesh['z'=16,'yh'=2,'yl'=2,'x'=4,'core'=2] {'yl','core'}, dimensions={0} | all-to-all | bytes 262144 | tf_op jit(solution)/shard_map/all_to_all | solution.py:727
  48.1 0.0 collective-permute-done.3.weights_far_ref
  48.1 0.0 copy-done.7
  48.1 0.0 copy-done.9
  48.1 0.0 copy-start.6
  48.2 1.2 %shard_map.91 = bf16[4,16,3072]{2,1,0:T(8,128)(2,1)S(1)} custom-call(bf16[4,64,256]{2,1,0:T(8,128)(2,1)S(1)} %all_to_all.15.parts_ref, f32[2,64]{1,0:T(2,128)S(1)} %copy-done.9, bf16[2,64,128]{2,1,0:T(8,128)(2,1)S(1)} %copy-done.7, bf16[6272,128]{1,0:T(8,128)(2,1)S(1)} %shard_map.88.weights_ref, bf16[6272,128]{1,0:T(8,128)(2,1)S(1)} %collective-permute-done.3.weights_far_ref), custom_call_target="tpu_custom_call" | custom-call | tf_op jit(solution)/shard_map/pallas_call | solution.py:613
  49.3 11.8 %all_to_all.16.shares_ref = bf16[4,16,3072]{2,1,0:T(8,128)(2,1)S(1)} all-to-all(bf16[4,16,3072]{2,1,0:T(8,128)(2,1)S(1)} %shard_map.91), channel_id=1, replica_groups=mesh['z'=16,'yh'=2,'yl'=2,'x'=4,'core'=2] {'x'}, dimensions={0} | all-to-all | bytes 786432 | tf_op jit(solution)/shard_map/all_to_all | solution.py:729
  61.1 0.0 copy-done.6
  61.1 0.7 %shard_map.92 = (bf16[16,1536]{1,0:T(8,128)(2,1)}, bf16[16,1536]{1,0:T(8,128)(2,1)}) custom-call(bf16[2,16,1536]{2,1,0:T(8,128)(2,1)S(1)} %get-tuple-element.35.rows_ref, f32[4,16,1536]{2,1,0:T(8,128)S(1)} %copy-done.6, bf16[4,16,3072]{2,1,0:T(8,128)(2,1)S(1)} %all_to_all.16.shares_ref), custom_call_target="tpu_custom_call" | custom-call | tf_op jit(solution)/shard_map/pallas_call | solution.py:677
  (1 shorter events, 0.0 us)
Async XLA Ops:
  0.6 12.8 %copy-start.2 = (bf16[128,1536]{1,0:T(8,128)(2,1)S(1)}, bf16[128,1536]{1,0:T(8,128)(2,1)}, u32[]{:S(2)}) copy-start(bf16[128,1536]{1,0:T(8,128)(2,1)} %tokens_ref.2) | copy-start | bytes 1179652
  0.6 12.8 %copy-start.3 = (bf16[128,1536]{1,0:T(8,128)(2,1)S(1)}, bf16[128,1536]{1,0:T(8,128)(2,1)}, u32[]{:S(2)}) copy-start(bf16[128,1536]{1,0:T(8,128)(2,1)} %cotangent_ref.2) | copy-start | bytes 1179652
  0.7 12.8 %copy-start.4 = (bf16[32,3,1536]{2,0,1:T(8,128)(2,1)S(1)}, bf16[32,3,1536]{2,0,1:T(8,128)(2,1)}, u32[]{:S(2)}) copy-start(bf16[32,3,1536]{2,0,1:T(8,128)(2,1)} %param.12) | copy-start | bytes 884740
  0.7 12.8 %copy-start.10 = (s32[32]{0:T(128)S(1)}, s32[32]{0:T(128)}, u32[]{:S(2)}) copy-start(s32[32]{0:T(128)} %counts_ref.7) | copy-start | bytes 388
  0.7 14.3 %copy-start = (bf16[1536,3,128]{2,0,1:T(8,128)(2,1)S(1)}, bf16[1536,3,128]{2,0,1:T(8,128)(2,1)}, u32[]{:S(2)}) copy-start(bf16[1536,3,128]{2,0,1:T(8,128)(2,1)} %param.9) | copy-start | bytes 3538948
  0.7 14.3 %copy-start.1 = (bf16[128,1536]{1,0:T(8,128)(2,1)S(1)}, bf16[128,1536]{1,0:T(8,128)(2,1)}, u32[]{:S(2)}) copy-start(bf16[128,1536]{1,0:T(8,128)(2,1)} %w_out_ref.2) | copy-start | bytes 1179652
  4.3 12.8 %all-to-all-start = ((bf16[4,128,256]{2,1,0:T(8,128)(2,1)}), bf16[4,128,256]{2,1,0:T(8,128)(2,1)S(1)}, u32[]{:S(2)}, u32[]{:S(2)}) async-start(bf16[4,128,256]{2,1,0:T(8,128)(2,1)} %get-tuple-element.26), calls=%async_computation | async-start | bytes 524288 | tf_op jit(solution)/shard_map/all_to_all | solution.py:704
  14.2 0.7 %copy-start.5 = (f32[4,16,1536]{2,1,0:T(8,128)}, f32[4,16,1536]{2,1,0:T(8,128)S(1)}, u32[]{:S(2)}) copy-start(f32[4,16,1536]{2,1,0:T(8,128)S(1)} %get-tuple-element.36.factors_ref) | copy-start | bytes 1179652
  15.0 0.8 %copy-start.8 = (bf16[2,64,128]{2,1,0:T(8,128)(2,1)S(1)}, bf16[2,64,128]{2,1,0:T(8,128)(2,1)}, u32[]{:S(2)}) copy-start(bf16[2,64,128]{2,1,0:T(8,128)(2,1)} %get-tuple-element.34.raw_ref) | copy-start | bytes 98308
  17.1 15.4 %collective-permute-start.1 = (bf16[512,256]{1,0:T(8,128)(2,1)S(1)}, bf16[512,256]{1,0:T(8,128)(2,1)S(1)}, u32[]{:S(2)}, u32[]{:S(2)}) collective-permute-start(bf16[512,256]{1,0:T(8,128)(2,1)S(1)} %bitcast.8), channel_id=1, source_target_pairs={{0,32},{64,96},{128,160},{192,224},{256,288},{320,352},{384,416},{... | collective-permute-start | bytes 786440 | tf_op jit(solution)/shard_map/ppermute | solution.py:710
  19.1 14.5 %collective-permute-start.2 = (bf16[512,256]{1,0:T(8,128)(2,1)S(1)}, bf16[512,256]{1,0:T(8,128)(2,1)S(1)}, u32[]{:S(2)}, u32[]{:S(2)}) collective-permute-start(bf16[512,256]{1,0:T(8,128)(2,1)S(1)} %bitcast.9), channel_id=1, source_target_pairs={{480,0},{32,64},{96,128},{160,192},{224,256},{288,320},{352,384},{... | collective-permute-start | bytes 786440 | tf_op jit(solution)/shard_map/ppermute | solution.py:710
  27.2 10.0 %collective-permute-start = (bf16[256,256]{1,0:T(8,128)(2,1)S(1)}, bf16[256,256]{1,0:T(8,128)(2,1)S(1)}, u32[]{:S(2)}, u32[]{:S(2)}) collective-permute-start(bf16[256,256]{1,0:T(8,128)(2,1)S(1)} %bitcast.11), channel_id=1, source_target_pairs={{448,0},{465,1},{80,16},{65,17},{480,32},{497,33},{112,48},{97,49}... | collective-permute-start | bytes 393224 | tf_op jit(solution)/shard_map/ppermute | solution.py:721
  30.6 17.6 %collective-permute-start.3 = (bf16[6272,128]{1,0:T(8,128)(2,1)S(1)}, bf16[6272,128]{1,0:T(8,128)(2,1)S(1)}, u32[]{:S(2)}, u32[]{:S(2)}) collective-permute-start(bf16[6272,128]{1,0:T(8,128)(2,1)S(1)} %shard_map.88.weights_ref), channel_id=1, source_target_pairs={{0,1},{1,0},{2,3},{3,2},{4,5},{5,4},{6,7},{7,6},{8,9},{9,8},{10,11... | collective-permute-start | bytes 4816904 | tf_op jit(solution)/shard_map/ppermute | solution.py:725
  37.2 10.9 %copy-start.7 = (bf16[2,64,128]{2,1,0:T(8,128)(2,1)S(1)}, bf16[2,64,128]{2,1,0:T(8,128)(2,1)}, u32[]{:S(2)}) copy-start(bf16[2,64,128]{2,1,0:T(8,128)(2,1)} %get-tuple-element.48.raw_ref) | copy-start | bytes 98308
  37.2 10.9 %copy-start.9 = (f32[2,64]{1,0:T(2,128)S(1)}, f32[2,64]{1,0:T(2,128)}, u32[]{:S(2)}) copy-start(f32[2,64]{1,0:T(2,128)} %gains_ref.3) | copy-start | bytes 1540
  48.1 13.0 %copy-start.6 = (f32[4,16,1536]{2,1,0:T(8,128)S(1)}, f32[4,16,1536]{2,1,0:T(8,128)}, u32[]{:S(2)}) copy-start(f32[4,16,1536]{2,1,0:T(8,128)} %copy-done.5) | copy-start | bytes 1179652
where the time goes:
time: 62.3 us; the launch traced here: 61.9 us
  starting transfers between devices  24.4 us (39%)
  blocking collectives  19.2 us (31%)
  Pallas kernels  14.4 us (23%)
  waiting for transfers between devices  1.55 us (2%)
  local copies, waits for them, and re-layouts  1.54 us (2%)
  between operations  0.83 us (1%)
    all_to_all x1, blocking collectives, per_device(): shares = lax.all_to_all(partial, 'x', 0, 0)  11.8 us
    ppermute x2, starting transfers between devices, per_device(): lax.ppermute(mine, 'z', pairs + [(j, i) for i, j in pairs])  10 us
    all_to_all x1, starting transfers between devices, per_device(): mine = lax.all_to_all(heads, ('yh', 'yl'), 0, 0)  9.08 us
    all_to_all x1, blocking collectives, per_device(): parts = lax.all_to_all(parts, ('yl', 'core'), 0, 0)  7.42 us
    pallas_call x1, Pallas kernels, attend_near(): pl.pallas_call(near_kernel, out_shape=(head_rows,) * 4 + (jax.ShapeDtypeS...  3.66 us
    pallas_call x1, Pallas kernels, enter(): pl.pallas_call(enter_kernel, out_shape=(jax.ShapeDtypeStruct((quad, rows,...  3.65 us
    pallas_call x1, Pallas kernels, attend_far(): pl.pallas_call(far_kernel, out_shape=jax.ShapeDtypeStruct((4, CHUNK // 4,...  3.5 us
    ppermute x1, starting transfers between devices, per_device(): lax.ppermute(far_half, ('z', 'yh', 'core'), [(far_source(i), i) for i in...  3.35 us
  transfers between devices with their start and end apart: 5, of which 2 were waited for; matrix products, arithmetic and copies ran while one was open for 0% of the time, Pallas kernels for 14%

commit v1 on v0

--- a/solution.py
+++ b/solution.py
@@ -276,11 +276,72 @@
     return top, total, jnp.sum(grads * shrink, axis=0, keepdims=True)
 
 
-def near_kernel(
+def early_kernel(
     counts_ref,
     first_ref,
     quad_ref,
+    qa_ref,
+    ka_ref,
+    va_ref,
+    da_ref,
+    kva_ref,
+    sa_ref,
+    ga_ref,
+    top_ref,
+):
+    half, _, starts, ends, _, _ = window_facts(counts_ref)
+    block_rows = CHUNK // 2
+    to_first = jnp.where(lax.rem(lax.axis_index("z"), 2) == 0, 2 * CHUNK, -2 * CHUNK)
+    for block in range(8):
+        at = slice(block * block_rows, (block + 1) * block_rows)
+        inner = slice(block % 4 * block_rows, (block % 4 + 1) * block_rows)
+        place = 2 * CHUNK + block % 4 * block_rows
+        stores = [ref.at[at, :] for ref in (qa_ref, ka_ref, va_ref, da_ref)]
+        stores.append(kva_ref.at[:, at])
+        if block < 4:
+            place_block(quad_ref.at[inner], place, starts, ends, stores)
+        else:
+            place_block(first_ref.at[inner], place + to_first, starts, ends, stores)
+
+    own_rows = pl.ds(pl.multiple_of(half * CHUNK, CHUNK), CHUNK)
+    q_own = qa_ref[own_rows, :]
+    d_own = da_ref[own_rows, :]
+    highest = jnp.full((8, CHUNK), -jnp.inf, F32)
+    for piece in range(4):
+        at = slice(piece * CHUNK, (piece + 1) * CHUNK)
+        scores = rows_dot(ka_ref[at, :], q_own)
+        sa_ref[at, :] = scores
+        highest = jnp.maximum(highest, rows_max(scores))
+        ga_ref[at, :] = rows_dot(va_ref[at, :], d_own)
+    top_ref[...] = highest
+
+
+def attend_early(counts, first, quad):
+    rows = 4 * CHUNK
+    head_rows = jax.ShapeDtypeStruct((rows, LANES), BF16)
+    scores = jax.ShapeDtypeStruct((rows, CHUNK), F32)
+    return pl.pallas_call(
+        early_kernel,
+        out_shape=(head_rows,) * 4
+        + (jax.ShapeDtypeStruct((LANES, rows), BF16), scores, scores)
+        + (jax.ShapeDtypeStruct((8, CHUNK), F32),),
+        in_specs=[SMEM] + [VMEM] * 2,
+        out_specs=(VMEM,) * 8,
+        compiler_params=pltpu.CompilerParams(vmem_limit_bytes=VMEM_LIMIT),
+    )(counts, first, quad)
+
+
+def near_kernel(
+    counts_ref,
     second_ref,
+    qa_ref,
+    ka_ref,
+    va_ref,
+    da_ref,
+    kva_ref,
+    sa_ref,
+    ga_ref,
+    top_ref,
     qx_ref,
     kx_ref,
     vx_ref,
@@ -296,27 +357,28 @@
 ):
     half, own_at, starts, ends, left_from, right_to = window_facts(counts_ref)
     block_rows = CHUNK // 2
-
-    def place(source, begin):
-        begin = pl.multiple_of(begin, block_rows)
+    even = lax.rem(lax.axis_index("z"), 2) == 0
+    first_at = pl.multiple_of(jnp.where(even, 4 * CHUNK, 0), 2 * CHUNK)
+    second_at = pl.multiple_of(jnp.where(even, 0, 4 * CHUNK), 2 * CHUNK)
+    early = ((qa_ref, qx_ref), (ka_ref, kx_ref), (va_ref, vx_ref), (da_ref, dx_ref))
+    for source, target in early:
+        target[2 * CHUNK : 4 * CHUNK, :] = source[0 : 2 * CHUNK, :]
+        target[pl.ds(first_at, 2 * CHUNK), :] = source[2 * CHUNK : 4 * CHUNK, :]
+    kv_ref[:, 2 * CHUNK : 4 * CHUNK] = kva_ref[:, 0 : 2 * CHUNK]
+    kv_ref[:, pl.ds(first_at, 2 * CHUNK)] = kva_ref[:, 2 * CHUNK : 4 * CHUNK]
+    for block in range(4):
+        inner = slice(block * block_rows, (block + 1) * block_rows)
+        begin = pl.multiple_of(second_at + block * block_rows, block_rows)
         at = pl.ds(begin, block_rows)
         stores = [ref.at[at, :] for ref in (qx_ref, kx_ref, vx_ref, dx_ref)]
-        place_block(source, begin, starts, ends, stores + [kv_ref.at[:, at]])
-
-    to_first = jnp.where(lax.rem(lax.axis_index("z"), 2) == 0, 2 * CHUNK, -2 * CHUNK)
-    for block in range(4):
-        at = slice(block * block_rows, (block + 1) * block_rows)
-        begin = 2 * CHUNK + block * block_rows
-        place(quad_ref.at[at], begin)
-        place(first_ref.at[at], begin + to_first)
-        place(second_ref.at[at], begin - to_first)
-
-    own_rows = pl.ds(pl.multiple_of(own_at, CHUNK), CHUNK)
-    q_own = qx_ref[own_rows, :]
-    d_own = dx_ref[own_rows, :]
-    highest = jnp.full((8, CHUNK), -jnp.inf, F32)
-    for piece in range(MAIN):
-        at = slice(piece * CHUNK, (piece + 1) * CHUNK)
+        place_block(second_ref.at[inner], begin, starts, ends, stores + [kv_ref.at[:, at]])
+
+    own_rows = pl.ds(pl.multiple_of(half * CHUNK, CHUNK), CHUNK)
+    q_own = qa_ref[own_rows, :]
+    d_own = da_ref[own_rows, :]
+    highest = top_ref[...]
+    for piece in range(2):
+        at = pl.ds(pl.multiple_of(second_at + piece * CHUNK, CHUNK), CHUNK)
         scores = rows_dot(kx_ref[at, :], q_own)
         so_ref[at, :] = scores
         highest = jnp.maximum(highest, rows_max(scores))
@@ -325,11 +387,24 @@
     total = jnp.zeros((8, CHUNK), F32)
     grads = jnp.zeros((8, CHUNK), F32)
     for piece in range(MAIN * CHUNK // TILE):
-        at = slice(piece * TILE, (piece + 1) * TILE)
-        weights = jnp.exp2(so_ref[at, :] * LOG2_E - highest)
-        so_ref[at, :] = weights
+        inner = piece * TILE
+        if inner < 2 * CHUNK:
+            to = pl.ds(2 * CHUNK + inner, TILE)
+        elif inner < 4 * CHUNK:
+            to = pl.ds(pl.multiple_of(first_at + inner - 2 * CHUNK, TILE), TILE)
+        else:
+            to = pl.ds(pl.multiple_of(second_at + inner - 4 * CHUNK, TILE), TILE)
+        if inner < 4 * CHUNK:
+            scores = sa_ref[inner : inner + TILE, :]
+            given = ga_ref[inner : inner + TILE, :]
+            go_ref[to, :] = given
+        else:
+            scores = so_ref[to, :]
+            given = go_ref[to, :]
+        weights = jnp.exp2(scores * LOG2_E - highest)
+        so_ref[to, :] = weights
         total = total + jnp.sum(by_eight(weights), axis=0)
-        grads = grads + jnp.sum(by_eight(weights * go_ref[at, :]), axis=0)
+        grads = grads + jnp.sum(by_eight(weights * given), axis=0)
     stats_ref[MAIN, 0:1, :] = highest
     stats_ref[MAIN, 1:2, :] = jnp.sum(total, axis=0, keepdims=True)
     stats_ref[MAIN, 2:3, :] = jnp.sum(grads, axis=0, keepdims=True)
@@ -361,7 +436,7 @@
     lax.fori_loop(0, MAIN - 1, one_chunk, 0)
 
 
-def attend_near(counts, first, quad, second):
+def attend_near(counts, second, early):
     rows = MAIN * CHUNK
     head_rows = jax.ShapeDtypeStruct((rows, LANES), BF16)
     scores = jax.ShapeDtypeStruct((rows, CHUNK), F32)
@@ -371,14 +446,14 @@
         out_shape=(head_rows,) * 4
         + (jax.ShapeDtypeStruct((LANES, rows), BF16),)
         + (scores, scores, tiles, tiles, jax.ShapeDtypeStruct((MAIN + 1, 8, CHUNK), F32)),
-        in_specs=[SMEM] + [VMEM] * 3,
+        in_specs=[SMEM] + [VMEM] * (1 + len(early)),
         out_specs=(VMEM,) * 10,
         scratch_shapes=[pltpu.VMEM((REACH_CHUNKS * CHUNK, CHUNK), F32)] * 2,
         cost_estimate=pl.CostEstimate(
             flops=9000000000, bytes_accessed=1 << 20, transcendentals=1 << 20
         ),
         compiler_params=pltpu.CompilerParams(vmem_limit_bytes=VMEM_LIMIT),
-    )(counts, first, quad, second)
+    )(counts, second, *early)
 
 
 def far_kernel(
@@ -721,7 +796,8 @@
     far = lax.ppermute(
         far_half, ("z", "yh", "core"), [(far_source(i), i) for i in range(halves)]
     )
-    near_parts = attend_near(image_counts, first, mine, second)
+    early = attend_early(image_counts, first, mine)
+    near_parts = attend_near(image_counts, second, early)
     weights_far = lax.ppermute(weights, "core", [(0, 1), (1, 0)])
     parts = attend_far(image_counts, far, near_parts)
     parts = lax.all_to_all(parts, ("yl", "core"), 0, 0)

time: 62.3 us -> 62.2 us (level)
  the two profiles are of different devices: /device:TPU:16 before, /device:TPU:8 now
where the time goes in v1:
time: 62.2 us; the launch traced here: 61.8 us
  starting transfers between devices  23.1 us (37%)
  blocking collectives  19 us (31%)
  Pallas kernels  13.6 us (22%)
  waiting for transfers between devices  3.7 us (6%)
  local copies, waits for them, and re-layouts  1.55 us (2%)
  between operations  0.83 us (1%)
    all_to_all x1, blocking collectives, per_device(): shares = lax.all_to_all(partial, 'x', 0, 0)  12.2 us
    ppermute x2, starting transfers between devices, per_device(): lax.ppermute(mine, 'z', pairs + [(j, i) for i, j in pairs])  10 us
    all_to_all x1, starting transfers between devices, per_device(): mine = lax.all_to_all(heads, ('yh', 'yl'), 0, 0)  9.19 us
    all_to_all x1, blocking collectives, per_device(): parts = lax.all_to_all(parts, ('yl', 'core'), 0, 0)  6.79 us
    pallas_call x1, Pallas kernels, enter(): pl.pallas_call(enter_kernel, out_shape=(jax.ShapeDtypeStruct((quad, rows,...  3.64 us
    pallas_call x1, Pallas kernels, attend_near(): pl.pallas_call(near_kernel, out_shape=(head_rows,) * 4 + (jax.ShapeDtypeS...  2.72 us
    pallas_call x1, Pallas kernels, attend_far(): pl.pallas_call(far_kernel, out_shape=jax.ShapeDtypeStruct((4, CHUNK // 4,...  2.52 us
    all_to_all x1, waiting for transfers between devices, per_device(): mine = lax.all_to_all(heads, ('yh', 'yl'), 0, 0)  2.05 us
  transfers between devices with their start and end apart: 5, of which 2 were waited for; matrix products, arithmetic and copies ran while one was open for 0% of the time, Pallas kernels for 13%

profile of v1, /device:TPU:8, one launch (start us, length us, event | category | flops | bytes accessed | tf_op | source)
XLA Modules:
  0.0 61.8 jit_solution(5622610826186727536)
XLA Ops:
  0.6 0.0 copy-start.2
  0.6 0.0 copy-start.3
  0.7 0.0 copy-start.4
  0.7 0.0 copy-start.9
  0.7 0.0 copy-start
  0.7 0.0 copy-start.1
  0.7 3.6 %shard_map.86 = (bf16[4,128,256]{2,1,0:T(8,128)(2,1)}, bf16[2,64,128]{2,1,0:T(8,128)(2,1)}, bf16[2,64,128]{2,1,0:T(8,128)(2,1)}) custom-call(s32[32]{0:T(128)} %counts_ref.9, f32[2,64]{1,0:T(2,128)} %gains_ref.3, bf16[128,1536]{1,0:T(8,128)(2,1)} %tokens_ref.2, bf16[128,1536]{1,0:T(8,128)(2,1)} %cotangent_ref.2, bf16[3,1536,128]{2,1,0:T(8,128)(2,1)} %bitcast.4, ...), custom_call_target="tpu_custom_call" | custom-call | tf_op jit(solution)/shard_map/pallas_call | solution.py:133
  4.3 9.2 %all-to-all-start = ((bf16[4,128,256]{2,1,0:T(8,128)(2,1)}), bf16[4,128,256]{2,1,0:T(8,128)(2,1)S(1)}, u32[]{:S(2)}, u32[]{:S(2)}) async-start(bf16[4,128,256]{2,1,0:T(8,128)(2,1)} %get-tuple-element.34), calls=%async_computation | async-start | bytes 524288 | tf_op jit(solution)/shard_map/all_to_all | solution.py:779
  13.5 0.0 copy-done.2
  13.5 0.0 copy-done.3
  13.5 0.0 copy-done.4
  13.5 0.0 copy-done.9
  13.5 0.8 %shard_map.87 = (bf16[2,16,1536]{2,1,0:T(8,128)(2,1)S(1)}, f32[4,16,1536]{2,1,0:T(8,128)S(1)}) custom-call(s32[32]{0:T(128)S(1)} %copy-done.9, bf16[128,1536]{1,0:T(8,128)(2,1)S(1)} %copy-done.2, bf16[128,1536]{1,0:T(8,128)(2,1)S(1)} %copy-done.3, bf16[3,32,1536]{2,1,0:T(8,128)(2,1)S(1)} %bitcast.10), custom_call_target="tpu_custom_call" | custom-call | tf_op jit(solution)/shard_map/pallas_call | solution.py:721
  14.3 0.0 copy-start.5
  14.3 0.7 %copy-done.5 = f32[4,16,1536]{2,1,0:T(8,128)} copy-done((f32[4,16,1536]{2,1,0:T(8,128)}, f32[4,16,1536]{2,1,0:T(8,128)S(1)}, u32[]{:S(2)}) %copy-start.5) | copy-done | bytes 393240
  15.1 0.0 copy-done
  15.1 0.0 copy-done.1
  15.1 0.0 copy-start.8
  15.1 0.8 %copy-done.8 = bf16[2,64,128]{2,1,0:T(8,128)(2,1)S(1)} copy-done((bf16[2,64,128]{2,1,0:T(8,128)(2,1)S(1)}, bf16[2,64,128]{2,1,0:T(8,128)(2,1)}, u32[]{:S(2)}) %copy-start.8) | copy-done | bytes 32792
  15.8 0.9 %shard_map.88.weights_ref = bf16[6272,128]{1,0:T(8,128)(2,1)S(1)} custom-call(bf16[3,1536,128]{2,1,0:T(8,128)(2,1)S(1)} %bitcast.5, bf16[128,1536]{1,0:T(8,128)(2,1)S(1)} %copy-done.1, bf16[2,64,128]{2,1,0:T(8,128)(2,1)S(1)} %copy-done.8), custom_call_target="tpu_custom_call" | custom-call | tf_op jit(solution)/shard_map/pallas_call | solution.py:169
  16.7 2.0 %all-to-all-done = bf16[4,128,256]{2,1,0:T(8,128)(2,1)S(1)} async-done(((bf16[4,128,256]{2,1,0:T(8,128)(2,1)}), bf16[4,128,256]{2,1,0:T(8,128)(2,1)S(1)}, u32[]{:S(2)}, u32[]{:S(2)}) %all-to-all-start) | async-done | bytes 262176 | tf_op jit(solution)/shard_map/all_to_all | solution.py:779
  18.7 1.9 %collective-permute-start.2 = (bf16[512,256]{1,0:T(8,128)(2,1)S(1)}, bf16[512,256]{1,0:T(8,128)(2,1)S(1)}, u32[]{:S(2)}, u32[]{:S(2)}) collective-permute-start(bf16[512,256]{1,0:T(8,128)(2,1)S(1)} %bitcast.6), channel_id=1, source_target_pairs={{0,32},{64,96},{128,160},{192,224},{256,288},{320,352},{384,416},{... | collective-permute-start | bytes 786440 | tf_op jit(solution)/shard_map/ppermute | solution.py:785
  20.7 8.1 %collective-permute-start.1 = (bf16[512,256]{1,0:T(8,128)(2,1)S(1)}, bf16[512,256]{1,0:T(8,128)(2,1)S(1)}, u32[]{:S(2)}, u32[]{:S(2)}) collective-permute-start(bf16[512,256]{1,0:T(8,128)(2,1)S(1)} %bitcast.7), channel_id=1, source_target_pairs={{480,0},{32,64},{96,128},{160,192},{224,256},{288,320},{352,384},{... | collective-permute-start | bytes 786440 | tf_op jit(solution)/shard_map/ppermute | solution.py:785
  28.8 1.9 %collective-permute-start = (bf16[256,256]{1,0:T(8,128)(2,1)S(1)}, bf16[256,256]{1,0:T(8,128)(2,1)S(1)}, u32[]{:S(2)}, u32[]{:S(2)}) collective-permute-start(bf16[256,256]{1,0:T(8,128)(2,1)S(1)} %bitcast.11), channel_id=1, source_target_pairs={{448,0},{465,1},{80,16},{65,17},{480,32},{497,33},{112,48},{97,49}... | collective-permute-start | bytes 393224 | tf_op jit(solution)/shard_map/ppermute | solution.py:796
  30.8 1.9 %collective-permute-start.3 = (bf16[6272,128]{1,0:T(8,128)(2,1)S(1)}, bf16[6272,128]{1,0:T(8,128)(2,1)S(1)}, u32[]{:S(2)}, u32[]{:S(2)}) collective-permute-start(bf16[6272,128]{1,0:T(8,128)(2,1)S(1)} %shard_map.88.weights_ref), channel_id=1, source_target_pairs={{0,1},{1,0},{2,3},{3,2},{4,5},{5,4},{6,7},{7,6},{8,9},{9,8},{10,11... | collective-permute-start | bytes 4816904 | tf_op jit(solution)/shard_map/ppermute | solution.py:801
  32.7 0.0 collective-permute-done.2.first_ref
  32.7 1.1 %shard_map.89 = (bf16[1024,128]{1,0:T(8,128)(2,1)S(1)}, bf16[1024,128]{1,0:T(8,128)(2,1)S(1)}, bf16[1024,128]{1,0:T(8,128)(2,1)S(1)}, bf16[1024,128]{1,0:T(8,128...) custom-call(s32[32]{0:T(128)S(1)} %copy-done.9, ...), custom_call_target="tpu_custom_call" | custom-call | tf_op jit(solution)/shard_map/pallas_call | solution.py:323
  33.8 1.6 %collective-permute-done.1.second_ref = bf16[512,256]{1,0:T(8,128)(2,1)S(1)} collective-permute-done((bf16[512,256]{1,0:T(8,128)(2,1)S(1)}, bf16[512,256]{1,0:T(8,128)(2,1)S(1)}, u32[]{:S(2)}, u32[]{:S(2)}) %collective-permute-start.1) | collective-permute-done | bytes 262176 | tf_op jit(solution)/shard_map/ppermute | solution.py:785
  35.5 2.7 %shard_map.90 = (bf16[1536,128]{1,0:T(8,128)(2,1)S(1)}, bf16[1536,128]{1,0:T(8,128)(2,1)S(1)}, bf16[1536,128]{1,0:T(8,128)(2,1)S(1)}, bf16[1536,128]{1,0:T(8,128...) custom-call(s32[32]{0:T(128)S(1)} %copy-done.9, ...), custom_call_target="tpu_custom_call" | custom-call | flops 8999999488 | bytes 1048576 | tf_op jit(solution)/shard_map/pallas_call | solution.py:444
  38.2 0.0 collective-permute-done.far_ref
  38.2 0.0 copy-start.7
  38.2 0.0 copy-start.10
  38.3 2.5 %shard_map.91 = bf16[4,64,256]{2,1,0:T(8,128)(2,1)S(1)} custom-call(s32[32]{0:T(128)S(1)} %copy-done.9, bf16[256,256]{1,0:T(8,128)(2,1)S(1)} %collective-permute-done.far_ref, bf16[1536,128]{1,0:T(8,128)(2,1)S(1)} %get-tuple-element.54.qx_ref, bf16[1536,128]{1,0:T(8,128)(2,1)S(1)} %get-tuple-element.55.kx_ref, ...), custom_call_target="tpu_custom_call" | custom-call | flops 8999999488 | bytes 1048576 | tf_op jit(solution)/shard_map/pallas_call | solution.py:618
  40.8 6.8 %all_to_all.15.parts_ref = bf16[4,64,256]{2,1,0:T(8,128)(2,1)S(1)} all-to-all(bf16[4,64,256]{2,1,0:T(8,128)(2,1)S(1)} %shard_map.91), channel_id=1, replica_groups=mesh['z'=16,'yh'=2,'yl'=2,'x'=4,'core'=2] {'yl','core'}, dimensions={0} | all-to-all | bytes 262144 | tf_op jit(solution)/shard_map/all_to_all | solution.py:803
  47.6 0.0 collective-permute-done.3.weights_far_ref
  47.6 0.0 copy-done.7
  47.6 0.0 copy-done.10
  47.6 0.0 copy-start.6
  47.6 1.2 %shard_map.92 = bf16[4,16,3072]{2,1,0:T(8,128)(2,1)S(1)} custom-call(bf16[4,64,256]{2,1,0:T(8,128)(2,1)S(1)} %all_to_all.15.parts_ref, f32[2,64]{1,0:T(2,128)S(1)} %copy-done.10, bf16[2,64,128]{2,1,0:T(8,128)(2,1)S(1)} %copy-done.7, bf16[6272,128]{1,0:T(8,128)(2,1)S(1)} %shard_map.88.weights_ref, bf16[6272,128]{1,0:T(8,128)(2,1)S(1)} %collective-permute-done.3.weights_far_ref), custom_call_target="tpu_custom_call" | custom-call | tf_op jit(solution)/shard_map/pallas_call | solution.py:688
  48.8 12.2 %all_to_all.16.shares_ref = bf16[4,16,3072]{2,1,0:T(8,128)(2,1)S(1)} all-to-all(bf16[4,16,3072]{2,1,0:T(8,128)(2,1)S(1)} %shard_map.92), channel_id=1, replica_groups=mesh['z'=16,'yh'=2,'yl'=2,'x'=4,'core'=2] {'x'}, dimensions={0} | all-to-all | bytes 786432 | tf_op jit(solution)/shard_map/all_to_all | solution.py:805
  61.0 0.0 copy-done.6
  61.0 0.7 %shard_map.93 = (bf16[16,1536]{1,0:T(8,128)(2,1)}, bf16[16,1536]{1,0:T(8,128)(2,1)}) custom-call(bf16[2,16,1536]{2,1,0:T(8,128)(2,1)S(1)} %get-tuple-element.43.rows_ref, f32[4,16,1536]{2,1,0:T(8,128)S(1)} %copy-done.6, bf16[4,16,3072]{2,1,0:T(8,128)(2,1)S(1)} %all_to_all.16.shares_ref), custom_call_target="tpu_custom_call" | custom-call | tf_op jit(solution)/shard_map/pallas_call | solution.py:752
  (1 shorter events, 0.0 us)
Async XLA Ops:
  0.6 12.9 %copy-start.2 = (bf16[128,1536]{1,0:T(8,128)(2,1)S(1)}, bf16[128,1536]{1,0:T(8,128)(2,1)}, u32[]{:S(2)}) copy-start(bf16[128,1536]{1,0:T(8,128)(2,1)} %tokens_ref.2) | copy-start | bytes 1179652
  0.6 12.9 %copy-start.3 = (bf16[128,1536]{1,0:T(8,128)(2,1)S(1)}, bf16[128,1536]{1,0:T(8,128)(2,1)}, u32[]{:S(2)}) copy-start(bf16[128,1536]{1,0:T(8,128)(2,1)} %cotangent_ref.2) | copy-start | bytes 1179652
  0.7 12.9 %copy-start.4 = (bf16[32,3,1536]{2,0,1:T(8,128)(2,1)S(1)}, bf16[32,3,1536]{2,0,1:T(8,128)(2,1)}, u32[]{:S(2)}) copy-start(bf16[32,3,1536]{2,0,1:T(8,128)(2,1)} %param.12) | copy-start | bytes 884740
  0.7 12.9 %copy-start.9 = (s32[32]{0:T(128)S(1)}, s32[32]{0:T(128)}, u32[]{:S(2)}) copy-start(s32[32]{0:T(128)} %counts_ref.9) | copy-start | bytes 388
  0.7 14.4 %copy-start = (bf16[1536,3,128]{2,0,1:T(8,128)(2,1)S(1)}, bf16[1536,3,128]{2,0,1:T(8,128)(2,1)}, u32[]{:S(2)}) copy-start(bf16[1536,3,128]{2,0,1:T(8,128)(2,1)} %param.9) | copy-start | bytes 3538948
  0.7 14.4 %copy-start.1 = (bf16[128,1536]{1,0:T(8,128)(2,1)S(1)}, bf16[128,1536]{1,0:T(8,128)(2,1)}, u32[]{:S(2)}) copy-start(bf16[128,1536]{1,0:T(8,128)(2,1)} %w_out_ref.2) | copy-start | bytes 1179652
  4.3 14.4 %all-to-all-start = ((bf16[4,128,256]{2,1,0:T(8,128)(2,1)}), bf16[4,128,256]{2,1,0:T(8,128)(2,1)S(1)}, u32[]{:S(2)}, u32[]{:S(2)}) async-start(bf16[4,128,256]{2,1,0:T(8,128)(2,1)} %get-tuple-element.34), calls=%async_computation | async-start | bytes 524288 | tf_op jit(solution)/shard_map/all_to_all | solution.py:779
  14.3 0.8 %copy-start.5 = (f32[4,16,1536]{2,1,0:T(8,128)}, f32[4,16,1536]{2,1,0:T(8,128)S(1)}, u32[]{:S(2)}) copy-start(f32[4,16,1536]{2,1,0:T(8,128)S(1)} %get-tuple-element.44.factors_ref) | copy-start | bytes 1179652
  15.1 0.8 %copy-start.8 = (bf16[2,64,128]{2,1,0:T(8,128)(2,1)S(1)}, bf16[2,64,128]{2,1,0:T(8,128)(2,1)}, u32[]{:S(2)}) copy-start(bf16[2,64,128]{2,1,0:T(8,128)(2,1)} %get-tuple-element.42.raw_ref) | copy-start | bytes 98308
  18.7 13.9 %collective-permute-start.2 = (bf16[512,256]{1,0:T(8,128)(2,1)S(1)}, bf16[512,256]{1,0:T(8,128)(2,1)S(1)}, u32[]{:S(2)}, u32[]{:S(2)}) collective-permute-start(bf16[512,256]{1,0:T(8,128)(2,1)S(1)} %bitcast.6), channel_id=1, source_target_pairs={{0,32},{64,96},{128,160},{192,224},{256,288},{320,352},{384,416},{... | collective-permute-start | bytes 786440 | tf_op jit(solution)/shard_map/ppermute | solution.py:785
  20.7 14.8 %collective-permute-start.1 = (bf16[512,256]{1,0:T(8,128)(2,1)S(1)}, bf16[512,256]{1,0:T(8,128)(2,1)S(1)}, u32[]{:S(2)}, u32[]{:S(2)}) collective-permute-start(bf16[512,256]{1,0:T(8,128)(2,1)S(1)} %bitcast.7), channel_id=1, source_target_pairs={{480,0},{32,64},{96,128},{160,192},{224,256},{288,320},{352,384},{... | collective-permute-start | bytes 786440 | tf_op jit(solution)/shard_map/ppermute | solution.py:785
  28.8 9.4 %collective-permute-start = (bf16[256,256]{1,0:T(8,128)(2,1)S(1)}, bf16[256,256]{1,0:T(8,128)(2,1)S(1)}, u32[]{:S(2)}, u32[]{:S(2)}) collective-permute-start(bf16[256,256]{1,0:T(8,128)(2,1)S(1)} %bitcast.11), channel_id=1, source_target_pairs={{448,0},{465,1},{80,16},{65,17},{480,32},{497,33},{112,48},{97,49}... | collective-permute-start | bytes 393224 | tf_op jit(solution)/shard_map/ppermute | solution.py:796
  30.8 16.8 %collective-permute-start.3 = (bf16[6272,128]{1,0:T(8,128)(2,1)S(1)}, bf16[6272,128]{1,0:T(8,128)(2,1)S(1)}, u32[]{:S(2)}, u32[]{:S(2)}) collective-permute-start(bf16[6272,128]{1,0:T(8,128)(2,1)S(1)} %shard_map.88.weights_ref), channel_id=1, source_target_pairs={{0,1},{1,0},{2,3},{3,2},{4,5},{5,4},{6,7},{7,6},{8,9},{9,8},{10,11... | collective-permute-start | bytes 4816904 | tf_op jit(solution)/shard_map/ppermute | solution.py:801
  38.2 9.3 %copy-start.7 = (bf16[2,64,128]{2,1,0:T(8,128)(2,1)S(1)}, bf16[2,64,128]{2,1,0:T(8,128)(2,1)}, u32[]{:S(2)}) copy-start(bf16[2,64,128]{2,1,0:T(8,128)(2,1)} %get-tuple-element.64.raw_ref) | copy-start | bytes 98308
  38.2 9.3 %copy-start.10 = (f32[2,64]{1,0:T(2,128)S(1)}, f32[2,64]{1,0:T(2,128)}, u32[]{:S(2)}) copy-start(f32[2,64]{1,0:T(2,128)} %gains_ref.3) | copy-start | bytes 1540
  47.6 13.4 %copy-start.6 = (f32[4,16,1536]{2,1,0:T(8,128)S(1)}, f32[4,16,1536]{2,1,0:T(8,128)}, u32[]{:S(2)}) copy-start(f32[4,16,1536]{2,1,0:T(8,128)} %copy-done.5) | copy-start | bytes 1179652

commit v2 on v1

--- a/solution.py
+++ b/solution.py
@@ -89,17 +89,28 @@
     raw_ref,
     raw_far_ref,
     rows_ref,
+    factors_ref,
+    hidden_ref,
+    d_mixed_ref,
 ):
     rows = tokens_ref.shape[0]
-    first = block_index() * rows
-    shift, scale, gate = modulation_rows(counts_ref, modulation_ref, first, rows)
-    normed, _ = layer_norm(tokens_ref[...].astype(F32))
-    hidden = (normed * (1.0 + scale) + shift).astype(BF16)
+    starts, ends = image_bounds(counts_ref, 0)
+    place = block_index() * rows + lax.broadcasted_iota(jnp.int32, (rows, LANES), 0)
+    member = ((place >= starts) & (place < ends)).astype(F32).astype(BF16)
+    member = member[:, : modulation_ref.shape[1]]
+    for part in range(3):
+        factors_ref[part] = jnp.dot(member, modulation_ref[part], preferred_element_type=F32)
+    for begin in range(0, rows, 16):
+        at = slice(begin, begin + 16)
+        normed, _ = layer_norm(tokens_ref[at, :].astype(F32))
+        hidden = normed * (1.0 + factors_ref[1, at, :]) + factors_ref[0, at, :]
+        hidden_ref[at, :] = hidden.astype(BF16)
+        d_mixed = cotangent_ref[at, :].astype(F32) * factors_ref[2, at, :]
+        d_mixed_ref[at, :] = d_mixed.astype(BF16)
     weights = jnp.concatenate([w_qkv_ref[part] for part in range(3)], axis=1)
-    qkv = jnp.dot(hidden, weights, preferred_element_type=F32)
+    qkv = jnp.dot(hidden_ref[...], weights, preferred_element_type=F32)
     q, k, v = (qkv[:, part * LANES : (part + 1) * LANES] for part in range(3))
-    d_mixed = (cotangent_ref[...].astype(F32) * gate).astype(BF16)
-    d_attn = rows_dot(d_mixed, w_out_ref[...])
+    d_attn = rows_dot(d_mixed_ref[...], w_out_ref[...])
     rows_ref[0] = q.astype(BF16)
     rows_ref[1] = k.astype(BF16)
     q = rows_ref[0].astype(F32)
@@ -135,7 +146,12 @@
         out_shape=(jax.ShapeDtypeStruct((quad, rows, 2 * LANES), BF16), raw, raw),
         in_specs=[SMEM] + [VMEM] * 6,
         out_specs=(VMEM,) * 3,
-        scratch_shapes=[pltpu.VMEM((2, rows, LANES), BF16)],
+        scratch_shapes=[
+            pltpu.VMEM((2, rows, LANES), BF16),
+            pltpu.VMEM((3,) + tokens.shape, F32),
+            pltpu.VMEM(tokens.shape, BF16),
+            pltpu.VMEM(tokens.shape, BF16),
+        ],
         compiler_params=pltpu.CompilerParams(vmem_limit_bytes=ENTER_LIMIT),
     )(counts, gains, tokens, cotangent, w_parts, w_out, modulation)
 

time: 62.2 us -> 62.3 us (level)
  no operation moved by 1% of the time
where the time goes in v2:
time: 62.3 us; the launch traced here: 61.6 us
  starting transfers between devices  23.1 us (37%)
  blocking collectives  19 us (30%)
  Pallas kernels  13.4 us (22%)
  waiting for transfers between devices  3.71 us (6%)
  local copies, waits for them, and re-layouts  1.55 us (2%)
  between operations  0.83 us (1%)
    all_to_all x1, blocking collectives, per_device(): shares = lax.all_to_all(partial, 'x', 0, 0)  12.2 us
    ppermute x2, starting transfers between devices, per_device(): lax.ppermute(mine, 'z', pairs + [(j, i) for i, j in pairs])  10 us
    all_to_all x1, starting transfers between devices, per_device(): mine = lax.all_to_all(heads, ('yh', 'yl'), 0, 0)  9.19 us
    all_to_all x1, blocking collectives, per_device(): parts = lax.all_to_all(parts, ('yl', 'core'), 0, 0)  6.79 us
    pallas_call x1, Pallas kernels, enter(): pl.pallas_call(enter_kernel, out_shape=(jax.ShapeDtypeStruct((quad, rows,...  3.51 us
    pallas_call x1, Pallas kernels, attend_near(): pl.pallas_call(near_kernel, out_shape=(head_rows,) * 4 + (jax.ShapeDtypeS...  2.72 us
    pallas_call x1, Pallas kernels, attend_far(): pl.pallas_call(far_kernel, out_shape=jax.ShapeDtypeStruct((4, CHUNK // 4,...  2.52 us
    all_to_all x1, waiting for transfers between devices, per_device(): mine = lax.all_to_all(heads, ('yh', 'yl'), 0, 0)  2.05 us
  transfers between devices with their start and end apart: 5, of which 2 were waited for; matrix products, arithmetic and copies ran while one was open for 0% of the time, Pallas kernels for 13%

profile of v2, /device:TPU:8, one launch (start us, length us, event | category | flops | bytes accessed | tf_op | source)
XLA Modules:
  0.0 61.6 jit_solution(12396503758502411590)
XLA Ops:
  0.6 0.0 copy-start.2
  0.6 0.0 copy-start.3
  0.7 0.0 copy-start.4
  0.7 0.0 copy-start.9
  0.7 0.0 copy-start
  0.7 0.0 copy-start.1
  0.7 3.5 %shard_map.86 = (bf16[4,128,256]{2,1,0:T(8,128)(2,1)}, bf16[2,64,128]{2,1,0:T(8,128)(2,1)}, bf16[2,64,128]{2,1,0:T(8,128)(2,1)}) custom-call(s32[32]{0:T(128)} %counts_ref.9, f32[2,64]{1,0:T(2,128)} %gains_ref.3, bf16[128,1536]{1,0:T(8,128)(2,1)} %tokens_ref.2, bf16[128,1536]{1,0:T(8,128)(2,1)} %cotangent_ref.2, bf16[3,1536,128]{2,1,0:T(8,128)(2,1)} %bitcast.4, ...), custom_call_target="tpu_custom_call" | custom-call | tf_op jit(solution)/shard_map/pallas_call | solution.py:144
  4.2 9.2 %all-to-all-start = ((bf16[4,128,256]{2,1,0:T(8,128)(2,1)}), bf16[4,128,256]{2,1,0:T(8,128)(2,1)S(1)}, u32[]{:S(2)}, u32[]{:S(2)}) async-start(bf16[4,128,256]{2,1,0:T(8,128)(2,1)} %get-tuple-element.34), calls=%async_computation | async-start | bytes 524288 | tf_op jit(solution)/shard_map/all_to_all | solution.py:795
  13.4 0.0 copy-done.2
  13.4 0.0 copy-done.3
  13.4 0.0 copy-done.4
  13.4 0.0 copy-done.9
  13.4 0.8 %shard_map.87 = (bf16[2,16,1536]{2,1,0:T(8,128)(2,1)S(1)}, f32[4,16,1536]{2,1,0:T(8,128)S(1)}) custom-call(s32[32]{0:T(128)S(1)} %copy-done.9, bf16[128,1536]{1,0:T(8,128)(2,1)S(1)} %copy-done.2, bf16[128,1536]{1,0:T(8,128)(2,1)S(1)} %copy-done.3, bf16[3,32,1536]{2,1,0:T(8,128)(2,1)S(1)} %bitcast.10), custom_call_target="tpu_custom_call" | custom-call | tf_op jit(solution)/shard_map/pallas_call | solution.py:737
  14.2 0.0 copy-start.5
  14.2 0.7 %copy-done.5 = f32[4,16,1536]{2,1,0:T(8,128)} copy-done((f32[4,16,1536]{2,1,0:T(8,128)}, f32[4,16,1536]{2,1,0:T(8,128)S(1)}, u32[]{:S(2)}) %copy-start.5) | copy-done | bytes 393240
  14.9 0.0 copy-done
  15.0 0.0 copy-done.1
  15.0 0.0 copy-start.8
  15.0 0.8 %copy-done.8 = bf16[2,64,128]{2,1,0:T(8,128)(2,1)S(1)} copy-done((bf16[2,64,128]{2,1,0:T(8,128)(2,1)S(1)}, bf16[2,64,128]{2,1,0:T(8,128)(2,1)}, u32[]{:S(2)}) %copy-start.8) | copy-done | bytes 32792
  15.7 0.9 %shard_map.88.weights_ref = bf16[6272,128]{1,0:T(8,128)(2,1)S(1)} custom-call(bf16[3,1536,128]{2,1,0:T(8,128)(2,1)S(1)} %bitcast.5, bf16[128,1536]{1,0:T(8,128)(2,1)S(1)} %copy-done.1, bf16[2,64,128]{2,1,0:T(8,128)(2,1)S(1)} %copy-done.8), custom_call_target="tpu_custom_call" | custom-call | tf_op jit(solution)/shard_map/pallas_call | solution.py:185
  16.6 2.0 %all-to-all-done = bf16[4,128,256]{2,1,0:T(8,128)(2,1)S(1)} async-done(((bf16[4,128,256]{2,1,0:T(8,128)(2,1)}), bf16[4,128,256]{2,1,0:T(8,128)(2,1)S(1)}, u32[]{:S(2)}, u32[]{:S(2)}) %all-to-all-start) | async-done | bytes 262176 | tf_op jit(solution)/shard_map/all_to_all | solution.py:795
  18.6 1.9 %collective-permute-start.2 = (bf16[512,256]{1,0:T(8,128)(2,1)S(1)}, bf16[512,256]{1,0:T(8,128)(2,1)S(1)}, u32[]{:S(2)}, u32[]{:S(2)}) collective-permute-start(bf16[512,256]{1,0:T(8,128)(2,1)S(1)} %bitcast.6), channel_id=1, source_target_pairs={{0,32},{64,96},{128,160},{192,224},{256,288},{320,352},{384,416},{... | collective-permute-start | bytes 786440 | tf_op jit(solution)/shard_map/ppermute | solution.py:801
  20.5 8.1 %collective-permute-start.1 = (bf16[512,256]{1,0:T(8,128)(2,1)S(1)}, bf16[512,256]{1,0:T(8,128)(2,1)S(1)}, u32[]{:S(2)}, u32[]{:S(2)}) collective-permute-start(bf16[512,256]{1,0:T(8,128)(2,1)S(1)} %bitcast.7), channel_id=1, source_target_pairs={{480,0},{32,64},{96,128},{160,192},{224,256},{288,320},{352,384},{... | collective-permute-start | bytes 786440 | tf_op jit(solution)/shard_map/ppermute | solution.py:801
  28.7 1.9 %collective-permute-start = (bf16[256,256]{1,0:T(8,128)(2,1)S(1)}, bf16[256,256]{1,0:T(8,128)(2,1)S(1)}, u32[]{:S(2)}, u32[]{:S(2)}) collective-permute-start(bf16[256,256]{1,0:T(8,128)(2,1)S(1)} %bitcast.11), channel_id=1, source_target_pairs={{448,0},{465,1},{80,16},{65,17},{480,32},{497,33},{112,48},{97,49}... | collective-permute-start | bytes 393224 | tf_op jit(solution)/shard_map/ppermute | solution.py:812
  30.6 1.9 %collective-permute-start.3 = (bf16[6272,128]{1,0:T(8,128)(2,1)S(1)}, bf16[6272,128]{1,0:T(8,128)(2,1)S(1)}, u32[]{:S(2)}, u32[]{:S(2)}) collective-permute-start(bf16[6272,128]{1,0:T(8,128)(2,1)S(1)} %shard_map.88.weights_ref), channel_id=1, source_target_pairs={{0,1},{1,0},{2,3},{3,2},{4,5},{5,4},{6,7},{7,6},{8,9},{9,8},{10,11... | collective-permute-start | bytes 4816904 | tf_op jit(solution)/shard_map/ppermute | solution.py:817
  32.5 0.0 collective-permute-done.2.first_ref
  32.6 1.1 %shard_map.89 = (bf16[1024,128]{1,0:T(8,128)(2,1)S(1)}, bf16[1024,128]{1,0:T(8,128)(2,1)S(1)}, bf16[1024,128]{1,0:T(8,128)(2,1)S(1)}, bf16[1024,128]{1,0:T(8,128...) custom-call(s32[32]{0:T(128)S(1)} %copy-done.9, ...), custom_call_target="tpu_custom_call" | custom-call | tf_op jit(solution)/shard_map/pallas_call | solution.py:339
  33.7 1.7 %collective-permute-done.1.second_ref = bf16[512,256]{1,0:T(8,128)(2,1)S(1)} collective-permute-done((bf16[512,256]{1,0:T(8,128)(2,1)S(1)}, bf16[512,256]{1,0:T(8,128)(2,1)S(1)}, u32[]{:S(2)}, u32[]{:S(2)}) %collective-permute-start.1) | collective-permute-done | bytes 262176 | tf_op jit(solution)/shard_map/ppermute | solution.py:801
  35.4 2.7 %shard_map.90 = (bf16[1536,128]{1,0:T(8,128)(2,1)S(1)}, bf16[1536,128]{1,0:T(8,128)(2,1)S(1)}, bf16[1536,128]{1,0:T(8,128)(2,1)S(1)}, bf16[1536,128]{1,0:T(8,128...) custom-call(s32[32]{0:T(128)S(1)} %copy-done.9, ...), custom_call_target="tpu_custom_call" | custom-call | flops 8999999488 | bytes 1048576 | tf_op jit(solution)/shard_map/pallas_call | solution.py:460
  38.1 0.0 collective-permute-done.far_ref
  38.1 0.0 copy-start.7
  38.1 0.0 copy-start.10
  38.1 2.5 %shard_map.91 = bf16[4,64,256]{2,1,0:T(8,128)(2,1)S(1)} custom-call(s32[32]{0:T(128)S(1)} %copy-done.9, bf16[256,256]{1,0:T(8,128)(2,1)S(1)} %collective-permute-done.far_ref, bf16[1536,128]{1,0:T(8,128)(2,1)S(1)} %get-tuple-element.54.qx_ref, bf16[1536,128]{1,0:T(8,128)(2,1)S(1)} %get-tuple-element.55.kx_ref, ...), custom_call_target="tpu_custom_call" | custom-call | flops 8999999488 | bytes 1048576 | tf_op jit(solution)/shard_map/pallas_call | solution.py:634
  40.6 6.8 %all_to_all.15.parts_ref = bf16[4,64,256]{2,1,0:T(8,128)(2,1)S(1)} all-to-all(bf16[4,64,256]{2,1,0:T(8,128)(2,1)S(1)} %shard_map.91), channel_id=1, replica_groups=mesh['z'=16,'yh'=2,'yl'=2,'x'=4,'core'=2] {'yl','core'}, dimensions={0} | all-to-all | bytes 262144 | tf_op jit(solution)/shard_map/all_to_all | solution.py:819
  47.4 0.0 collective-permute-done.3.weights_far_ref
  47.4 0.0 copy-done.7
  47.4 0.0 copy-done.10
  47.4 0.0 copy-start.6
  47.4 1.2 %shard_map.92 = bf16[4,16,3072]{2,1,0:T(8,128)(2,1)S(1)} custom-call(bf16[4,64,256]{2,1,0:T(8,128)(2,1)S(1)} %all_to_all.15.parts_ref, f32[2,64]{1,0:T(2,128)S(1)} %copy-done.10, bf16[2,64,128]{2,1,0:T(8,128)(2,1)S(1)} %copy-done.7, bf16[6272,128]{1,0:T(8,128)(2,1)S(1)} %shard_map.88.weights_ref, bf16[6272,128]{1,0:T(8,128)(2,1)S(1)} %collective-permute-done.3.weights_far_ref), custom_call_target="tpu_custom_call" | custom-call | tf_op jit(solution)/shard_map/pallas_call | solution.py:704
  48.6 12.2 %all_to_all.16.shares_ref = bf16[4,16,3072]{2,1,0:T(8,128)(2,1)S(1)} all-to-all(bf16[4,16,3072]{2,1,0:T(8,128)(2,1)S(1)} %shard_map.92), channel_id=1, replica_groups=mesh['z'=16,'yh'=2,'yl'=2,'x'=4,'core'=2] {'x'}, dimensions={0} | all-to-all | bytes 786432 | tf_op jit(solution)/shard_map/all_to_all | solution.py:821
  60.9 0.0 copy-done.6
  60.9 0.7 %shard_map.93 = (bf16[16,1536]{1,0:T(8,128)(2,1)}, bf16[16,1536]{1,0:T(8,128)(2,1)}) custom-call(bf16[2,16,1536]{2,1,0:T(8,128)(2,1)S(1)} %get-tuple-element.43.rows_ref, f32[4,16,1536]{2,1,0:T(8,128)S(1)} %copy-done.6, bf16[4,16,3072]{2,1,0:T(8,128)(2,1)S(1)} %all_to_all.16.shares_ref), custom_call_target="tpu_custom_call" | custom-call | tf_op jit(solution)/shard_map/pallas_call | solution.py:768
  (1 shorter events, 0.0 us)
Async XLA Ops:
  0.6 12.8 %copy-start.2 = (bf16[128,1536]{1,0:T(8,128)(2,1)S(1)}, bf16[128,1536]{1,0:T(8,128)(2,1)}, u32[]{:S(2)}) copy-start(bf16[128,1536]{1,0:T(8,128)(2,1)} %tokens_ref.2) | copy-start | bytes 1179652
  0.6 12.8 %copy-start.3 = (bf16[128,1536]{1,0:T(8,128)(2,1)S(1)}, bf16[128,1536]{1,0:T(8,128)(2,1)}, u32[]{:S(2)}) copy-start(bf16[128,1536]{1,0:T(8,128)(2,1)} %cotangent_ref.2) | copy-start | bytes 1179652
  0.7 12.8 %copy-start.4 = (bf16[32,3,1536]{2,0,1:T(8,128)(2,1)S(1)}, bf16[32,3,1536]{2,0,1:T(8,128)(2,1)}, u32[]{:S(2)}) copy-start(bf16[32,3,1536]{2,0,1:T(8,128)(2,1)} %param.12) | copy-start | bytes 884740
  0.7 12.7 %copy-start.9 = (s32[32]{0:T(128)S(1)}, s32[32]{0:T(128)}, u32[]{:S(2)}) copy-start(s32[32]{0:T(128)} %counts_ref.9) | copy-start | bytes 388
  0.7 14.3 %copy-start = (bf16[1536,3,128]{2,0,1:T(8,128)(2,1)S(1)}, bf16[1536,3,128]{2,0,1:T(8,128)(2,1)}, u32[]{:S(2)}) copy-start(bf16[1536,3,128]{2,0,1:T(8,128)(2,1)} %param.9) | copy-start | bytes 3538948
  0.7 14.3 %copy-start.1 = (bf16[128,1536]{1,0:T(8,128)(2,1)S(1)}, bf16[128,1536]{1,0:T(8,128)(2,1)}, u32[]{:S(2)}) copy-start(bf16[128,1536]{1,0:T(8,128)(2,1)} %w_out_ref.2) | copy-start | bytes 1179652
  4.2 14.4 %all-to-all-start = ((bf16[4,128,256]{2,1,0:T(8,128)(2,1)}), bf16[4,128,256]{2,1,0:T(8,128)(2,1)S(1)}, u32[]{:S(2)}, u32[]{:S(2)}) async-start(bf16[4,128,256]{2,1,0:T(8,128)(2,1)} %get-tuple-element.34), calls=%async_computation | async-start | bytes 524288 | tf_op jit(solution)/shard_map/all_to_all | solution.py:795
  14.2 0.8 %copy-start.5 = (f32[4,16,1536]{2,1,0:T(8,128)}, f32[4,16,1536]{2,1,0:T(8,128)S(1)}, u32[]{:S(2)}) copy-start(f32[4,16,1536]{2,1,0:T(8,128)S(1)} %get-tuple-element.44.factors_ref) | copy-start | bytes 1179652
  15.0 0.8 %copy-start.8 = (bf16[2,64,128]{2,1,0:T(8,128)(2,1)S(1)}, bf16[2,64,128]{2,1,0:T(8,128)(2,1)}, u32[]{:S(2)}) copy-start(bf16[2,64,128]{2,1,0:T(8,128)(2,1)} %get-tuple-element.42.raw_ref) | copy-start | bytes 98308
  18.6 13.9 %collective-permute-start.2 = (bf16[512,256]{1,0:T(8,128)(2,1)S(1)}, bf16[512,256]{1,0:T(8,128)(2,1)S(1)}, u32[]{:S(2)}, u32[]{:S(2)}) collective-permute-start(bf16[512,256]{1,0:T(8,128)(2,1)S(1)} %bitcast.6), channel_id=1, source_target_pairs={{0,32},{64,96},{128,160},{192,224},{256,288},{320,352},{384,416},{... | collective-permute-start | bytes 786440 | tf_op jit(solution)/shard_map/ppermute | solution.py:801
  20.5 14.8 %collective-permute-start.1 = (bf16[512,256]{1,0:T(8,128)(2,1)S(1)}, bf16[512,256]{1,0:T(8,128)(2,1)S(1)}, u32[]{:S(2)}, u32[]{:S(2)}) collective-permute-start(bf16[512,256]{1,0:T(8,128)(2,1)S(1)} %bitcast.7), channel_id=1, source_target_pairs={{480,0},{32,64},{96,128},{160,192},{224,256},{288,320},{352,384},{... | collective-permute-start | bytes 786440 | tf_op jit(solution)/shard_map/ppermute | solution.py:801
  28.7 9.4 %collective-permute-start = (bf16[256,256]{1,0:T(8,128)(2,1)S(1)}, bf16[256,256]{1,0:T(8,128)(2,1)S(1)}, u32[]{:S(2)}, u32[]{:S(2)}) collective-permute-start(bf16[256,256]{1,0:T(8,128)(2,1)S(1)} %bitcast.11), channel_id=1, source_target_pairs={{448,0},{465,1},{80,16},{65,17},{480,32},{497,33},{112,48},{97,49}... | collective-permute-start | bytes 393224 | tf_op jit(solution)/shard_map/ppermute | solution.py:812
  30.6 16.8 %collective-permute-start.3 = (bf16[6272,128]{1,0:T(8,128)(2,1)S(1)}, bf16[6272,128]{1,0:T(8,128)(2,1)S(1)}, u32[]{:S(2)}, u32[]{:S(2)}) collective-permute-start(bf16[6272,128]{1,0:T(8,128)(2,1)S(1)} %shard_map.88.weights_ref), channel_id=1, source_target_pairs={{0,1},{1,0},{2,3},{3,2},{4,5},{5,4},{6,7},{7,6},{8,9},{9,8},{10,11... | collective-permute-start | bytes 4816904 | tf_op jit(solution)/shard_map/ppermute | solution.py:817
  38.1 9.3 %copy-start.7 = (bf16[2,64,128]{2,1,0:T(8,128)(2,1)S(1)}, bf16[2,64,128]{2,1,0:T(8,128)(2,1)}, u32[]{:S(2)}) copy-start(bf16[2,64,128]{2,1,0:T(8,128)(2,1)} %get-tuple-element.64.raw_ref) | copy-start | bytes 98308
  38.1 9.3 %copy-start.10 = (f32[2,64]{1,0:T(2,128)S(1)}, f32[2,64]{1,0:T(2,128)}, u32[]{:S(2)}) copy-start(f32[2,64]{1,0:T(2,128)} %gains_ref.3) | copy-start | bytes 1540
  47.4 13.4 %copy-start.6 = (f32[4,16,1536]{2,1,0:T(8,128)S(1)}, f32[4,16,1536]{2,1,0:T(8,128)}, u32[]{:S(2)}) copy-start(f32[4,16,1536]{2,1,0:T(8,128)} %copy-done.5) | copy-start | bytes 1179652

commit v3 on v2

--- a/solution.py
+++ b/solution.py
@@ -801,13 +801,15 @@
         lax.ppermute(mine, "z", pairs + [(j, i) for i, j in pairs]) for pairs in swaps
     )
     halves = 4 * z_count
+    crosses = (lax.rem(lax.axis_index("z"), 2) == lax.axis_index("core")).astype(jnp.int32)
     far_half = jnp.where(
-        lax.axis_index("yh") == lax.axis_index("core"), mine[pair_rows:], mine[:pair_rows]
+        lax.axis_index("yh") == crosses, mine[pair_rows:], mine[:pair_rows]
     )
 
     def far_source(target):
         z, yh, core = target // 4, target // 2 % 2, target % 2
-        return (z + (2 if yh else -2)) % z_count * 4 + (yh ^ core) * 2 + core
+        other = yh ^ int(z % 2 == core)
+        return (z + (2 if yh else -2)) % z_count * 4 + other * 2 + core
 
     far = lax.ppermute(
         far_half, ("z", "yh", "core"), [(far_source(i), i) for i in range(halves)]

time: 62.3 us -> 64.1 us (1.029)
  starting transfers between devices: 23.1 us -> 25.4 us
    ppermute x1, starting transfers between devices: 1.92 us -> 4.26 us  [per_device(): lax.ppermute(far_half, ('z', 'yh', 'core'), [(far_source(i), i) for i in...]
    ppermute x2, waiting for transfers between devices: 1.66 us -> 0.01 us  [per_device(): lax.ppermute(mine, 'z', pairs + [(j, i) for i, j in pairs])]
    ppermute x1, waiting for transfers between devices: 0.01 us -> 1.22 us  [per_device(): lax.ppermute(far_half, ('z', 'yh', 'core'), [(far_source(i), i) for i in...]
where the time goes in v3:
time: 64.1 us; the launch traced here: 63.6 us
  starting transfers between devices  25.4 us (40%)
  blocking collectives  19.1 us (30%)
  Pallas kernels  13.5 us (21%)
  waiting for transfers between devices  3.27 us (5%)
  local copies, waits for them, and re-layouts  1.54 us (2%)
  between operations  0.82 us (1%)
    all_to_all x1, blocking collectives, per_device(): shares = lax.all_to_all(partial, 'x', 0, 0)  12.2 us
    ppermute x2, starting transfers between devices, per_device(): lax.ppermute(mine, 'z', pairs + [(j, i) for i, j in pairs])  10 us
    all_to_all x1, starting transfers between devices, per_device(): mine = lax.all_to_all(heads, ('yh', 'yl'), 0, 0)  9.19 us
    all_to_all x1, blocking collectives, per_device(): parts = lax.all_to_all(parts, ('yl', 'core'), 0, 0)  6.81 us
    ppermute x1, starting transfers between devices, per_device(): lax.ppermute(far_half, ('z', 'yh', 'core'), [(far_source(i), i) for i in...  4.26 us
    pallas_call x1, Pallas kernels, enter(): pl.pallas_call(enter_kernel, out_shape=(jax.ShapeDtypeStruct((quad, rows,...  3.51 us
    pallas_call x1, Pallas kernels, attend_near(): pl.pallas_call(near_kernel, out_shape=(head_rows,) * 4 + (jax.ShapeDtypeS...  2.78 us
    pallas_call x1, Pallas kernels, attend_far(): pl.pallas_call(far_kernel, out_shape=jax.ShapeDtypeStruct((4, CHUNK // 4,...  2.55 us
  transfers between devices with their start and end apart: 5, of which 2 were waited for; matrix products, arithmetic and copies ran while one was open for 0% of the time, Pallas kernels for 13%

profile of v3, /device:TPU:8, one launch (start us, length us, event | category | flops | bytes accessed | tf_op | source)
XLA Modules:
  0.0 63.6 jit_solution(18296519011030315160)
XLA Ops:
  0.6 0.0 copy-start.2
  0.6 0.0 copy-start.3
  0.7 0.0 copy-start.4
  0.7 0.0 copy-start.9
  0.7 0.0 copy-start
  0.7 0.0 copy-start.1
  0.7 3.5 %shard_map.86 = (bf16[4,128,256]{2,1,0:T(8,128)(2,1)}, bf16[2,64,128]{2,1,0:T(8,128)(2,1)}, bf16[2,64,128]{2,1,0:T(8,128)(2,1)}) custom-call(s32[32]{0:T(128)} %counts_ref.9, f32[2,64]{1,0:T(2,128)} %gains_ref.3, bf16[128,1536]{1,0:T(8,128)(2,1)} %tokens_ref.2, bf16[128,1536]{1,0:T(8,128)(2,1)} %cotangent_ref.2, bf16[3,1536,128]{2,1,0:T(8,128)(2,1)} %bitcast.4, ...), custom_call_target="tpu_custom_call" | custom-call | tf_op jit(solution)/shard_map/pallas_call | solution.py:144
  4.2 9.2 %all-to-all-start = ((bf16[4,128,256]{2,1,0:T(8,128)(2,1)}), bf16[4,128,256]{2,1,0:T(8,128)(2,1)S(1)}, u32[]{:S(2)}, u32[]{:S(2)}) async-start(bf16[4,128,256]{2,1,0:T(8,128)(2,1)} %get-tuple-element.34), calls=%async_computation | async-start | bytes 524288 | tf_op jit(solution)/shard_map/all_to_all | solution.py:795
  13.4 0.0 copy-done.2
  13.4 0.0 copy-done.3
  13.4 0.0 copy-done.4
  13.4 0.0 copy-done.9
  13.4 0.8 %shard_map.87 = (bf16[2,16,1536]{2,1,0:T(8,128)(2,1)S(1)}, f32[4,16,1536]{2,1,0:T(8,128)S(1)}) custom-call(s32[32]{0:T(128)S(1)} %copy-done.9, bf16[128,1536]{1,0:T(8,128)(2,1)S(1)} %copy-done.2, bf16[128,1536]{1,0:T(8,128)(2,1)S(1)} %copy-done.3, bf16[3,32,1536]{2,1,0:T(8,128)(2,1)S(1)} %bitcast.10), custom_call_target="tpu_custom_call" | custom-call | tf_op jit(solution)/shard_map/pallas_call | solution.py:737
  14.2 0.0 copy-start.5
  14.2 0.7 %copy-done.5 = f32[4,16,1536]{2,1,0:T(8,128)} copy-done((f32[4,16,1536]{2,1,0:T(8,128)}, f32[4,16,1536]{2,1,0:T(8,128)S(1)}, u32[]{:S(2)}) %copy-start.5) | copy-done | bytes 393240
  14.9 0.0 copy-done
  15.0 0.0 copy-done.1
  15.0 0.0 copy-start.8
  15.0 0.8 %copy-done.8 = bf16[2,64,128]{2,1,0:T(8,128)(2,1)S(1)} copy-done((bf16[2,64,128]{2,1,0:T(8,128)(2,1)S(1)}, bf16[2,64,128]{2,1,0:T(8,128)(2,1)}, u32[]{:S(2)}) %copy-start.8) | copy-done | bytes 32792
  15.7 0.9 %shard_map.88.weights_ref = bf16[6272,128]{1,0:T(8,128)(2,1)S(1)} custom-call(bf16[3,1536,128]{2,1,0:T(8,128)(2,1)S(1)} %bitcast.5, bf16[128,1536]{1,0:T(8,128)(2,1)S(1)} %copy-done.1, bf16[2,64,128]{2,1,0:T(8,128)(2,1)S(1)} %copy-done.8), custom_call_target="tpu_custom_call" | custom-call | tf_op jit(solution)/shard_map/pallas_call | solution.py:185
  16.6 2.0 %all-to-all-done = bf16[4,128,256]{2,1,0:T(8,128)(2,1)S(1)} async-done(((bf16[4,128,256]{2,1,0:T(8,128)(2,1)}), bf16[4,128,256]{2,1,0:T(8,128)(2,1)S(1)}, u32[]{:S(2)}, u32[]{:S(2)}) %all-to-all-start) | async-done | bytes 262176 | tf_op jit(solution)/shard_map/all_to_all | solution.py:795
  18.6 1.9 %collective-permute-start.2 = (bf16[512,256]{1,0:T(8,128)(2,1)S(1)}, bf16[512,256]{1,0:T(8,128)(2,1)S(1)}, u32[]{:S(2)}, u32[]{:S(2)}) collective-permute-start(bf16[512,256]{1,0:T(8,128)(2,1)S(1)} %bitcast.6), channel_id=1, source_target_pairs={{0,32},{64,96},{128,160},{192,224},{256,288},{320,352},{384,416},{... | collective-permute-start | bytes 786440 | tf_op jit(solution)/shard_map/ppermute | solution.py:801
  20.5 8.1 %collective-permute-start.1 = (bf16[512,256]{1,0:T(8,128)(2,1)S(1)}, bf16[512,256]{1,0:T(8,128)(2,1)S(1)}, u32[]{:S(2)}, u32[]{:S(2)}) collective-permute-start(bf16[512,256]{1,0:T(8,128)(2,1)S(1)} %bitcast.7), channel_id=1, source_target_pairs={{480,0},{32,64},{96,128},{160,192},{224,256},{288,320},{352,384},{... | collective-permute-start | bytes 786440 | tf_op jit(solution)/shard_map/ppermute | solution.py:801
  28.7 4.3 %collective-permute-start = (bf16[256,256]{1,0:T(8,128)(2,1)S(1)}, bf16[256,256]{1,0:T(8,128)(2,1)S(1)}, u32[]{:S(2)}, u32[]{:S(2)}) collective-permute-start(bf16[256,256]{1,0:T(8,128)(2,1)S(1)} %bitcast.11), channel_id=1, source_target_pairs={{464,0},{449,1},{64,16},{81,17},{480,32},{497,33},{112,48},{97,49}... | collective-permute-start | bytes 393224 | tf_op jit(solution)/shard_map/ppermute | solution.py:814
  33.0 1.9 %collective-permute-start.3 = (bf16[6272,128]{1,0:T(8,128)(2,1)S(1)}, bf16[6272,128]{1,0:T(8,128)(2,1)S(1)}, u32[]{:S(2)}, u32[]{:S(2)}) collective-permute-start(bf16[6272,128]{1,0:T(8,128)(2,1)S(1)} %shard_map.88.weights_ref), channel_id=1, source_target_pairs={{0,1},{1,0},{2,3},{3,2},{4,5},{5,4},{6,7},{7,6},{8,9},{9,8},{10,11... | collective-permute-start | bytes 4816904 | tf_op jit(solution)/shard_map/ppermute | solution.py:819
  34.9 0.0 collective-permute-done.2.first_ref
  34.9 1.1 %shard_map.89 = (bf16[1024,128]{1,0:T(8,128)(2,1)S(1)}, bf16[1024,128]{1,0:T(8,128)(2,1)S(1)}, bf16[1024,128]{1,0:T(8,128)(2,1)S(1)}, bf16[1024,128]{1,0:T(8,128...) custom-call(s32[32]{0:T(128)S(1)} %copy-done.9, ...), custom_call_target="tpu_custom_call" | custom-call | tf_op jit(solution)/shard_map/pallas_call | solution.py:339
  36.0 0.0 collective-permute-done.1.second_ref
  36.1 2.8 %shard_map.90 = (bf16[1536,128]{1,0:T(8,128)(2,1)S(1)}, bf16[1536,128]{1,0:T(8,128)(2,1)S(1)}, bf16[1536,128]{1,0:T(8,128)(2,1)S(1)}, bf16[1536,128]{1,0:T(8,128...) custom-call(s32[32]{0:T(128)S(1)} %copy-done.9, ...), custom_call_target="tpu_custom_call" | custom-call | flops 8999999488 | bytes 1048576 | tf_op jit(solution)/shard_map/pallas_call | solution.py:460
  38.8 1.2 %collective-permute-done.far_ref = bf16[256,256]{1,0:T(8,128)(2,1)S(1)} collective-permute-done((bf16[256,256]{1,0:T(8,128)(2,1)S(1)}, bf16[256,256]{1,0:T(8,128)(2,1)S(1)}, u32[]{:S(2)}, u32[]{:S(2)}) %collective-permute-start) | collective-permute-done | bytes 131104 | tf_op jit(solution)/shard_map/ppermute | solution.py:814
  40.1 0.0 copy-start.7
  40.1 0.0 copy-start.10
  40.1 2.5 %shard_map.91 = bf16[4,64,256]{2,1,0:T(8,128)(2,1)S(1)} custom-call(s32[32]{0:T(128)S(1)} %copy-done.9, bf16[256,256]{1,0:T(8,128)(2,1)S(1)} %collective-permute-done.far_ref, bf16[1536,128]{1,0:T(8,128)(2,1)S(1)} %get-tuple-element.54.qx_ref, bf16[1536,128]{1,0:T(8,128)(2,1)S(1)} %get-tuple-element.55.kx_ref, ...), custom_call_target="tpu_custom_call" | custom-call | flops 8999999488 | bytes 1048576 | tf_op jit(solution)/shard_map/pallas_call | solution.py:634
  42.6 6.8 %all_to_all.15.parts_ref = bf16[4,64,256]{2,1,0:T(8,128)(2,1)S(1)} all-to-all(bf16[4,64,256]{2,1,0:T(8,128)(2,1)S(1)} %shard_map.91), channel_id=1, replica_groups=mesh['z'=16,'yh'=2,'yl'=2,'x'=4,'core'=2] {'yl','core'}, dimensions={0} | all-to-all | bytes 262144 | tf_op jit(solution)/shard_map/all_to_all | solution.py:821
  49.4 0.0 collective-permute-done.3.weights_far_ref
  49.4 0.0 copy-done.7
  49.4 0.0 copy-done.10
  49.4 0.0 copy-start.6
  49.5 1.2 %shard_map.92 = bf16[4,16,3072]{2,1,0:T(8,128)(2,1)S(1)} custom-call(bf16[4,64,256]{2,1,0:T(8,128)(2,1)S(1)} %all_to_all.15.parts_ref, f32[2,64]{1,0:T(2,128)S(1)} %copy-done.10, bf16[2,64,128]{2,1,0:T(8,128)(2,1)S(1)} %copy-done.7, bf16[6272,128]{1,0:T(8,128)(2,1)S(1)} %shard_map.88.weights_ref, bf16[6272,128]{1,0:T(8,128)(2,1)S(1)} %collective-permute-done.3.weights_far_ref), custom_call_target="tpu_custom_call" | custom-call | tf_op jit(solution)/shard_map/pallas_call | solution.py:704
  50.6 12.2 %all_to_all.16.shares_ref = bf16[4,16,3072]{2,1,0:T(8,128)(2,1)S(1)} all-to-all(bf16[4,16,3072]{2,1,0:T(8,128)(2,1)S(1)} %shard_map.92), channel_id=1, replica_groups=mesh['z'=16,'yh'=2,'yl'=2,'x'=4,'core'=2] {'x'}, dimensions={0} | all-to-all | bytes 786432 | tf_op jit(solution)/shard_map/all_to_all | solution.py:823
  62.9 0.0 copy-done.6
  62.9 0.7 %shard_map.93 = (bf16[16,1536]{1,0:T(8,128)(2,1)}, bf16[16,1536]{1,0:T(8,128)(2,1)}) custom-call(bf16[2,16,1536]{2,1,0:T(8,128)(2,1)S(1)} %get-tuple-element.43.rows_ref, f32[4,16,1536]{2,1,0:T(8,128)S(1)} %copy-done.6, bf16[4,16,3072]{2,1,0:T(8,128)(2,1)S(1)} %all_to_all.16.shares_ref), custom_call_target="tpu_custom_call" | custom-call | tf_op jit(solution)/shard_map/pallas_call | solution.py:768
  (1 shorter events, 0.0 us)
Async XLA Ops:
  0.6 12.8 %copy-start.2 = (bf16[128,1536]{1,0:T(8,128)(2,1)S(1)}, bf16[128,1536]{1,0:T(8,128)(2,1)}, u32[]{:S(2)}) copy-start(bf16[128,1536]{1,0:T(8,128)(2,1)} %tokens_ref.2) | copy-start | bytes 1179652
  0.6 12.8 %copy-start.3 = (bf16[128,1536]{1,0:T(8,128)(2,1)S(1)}, bf16[128,1536]{1,0:T(8,128)(2,1)}, u32[]{:S(2)}) copy-start(bf16[128,1536]{1,0:T(8,128)(2,1)} %cotangent_ref.2) | copy-start | bytes 1179652
  0.7 12.8 %copy-start.4 = (bf16[32,3,1536]{2,0,1:T(8,128)(2,1)S(1)}, bf16[32,3,1536]{2,0,1:T(8,128)(2,1)}, u32[]{:S(2)}) copy-start(bf16[32,3,1536]{2,0,1:T(8,128)(2,1)} %param.12) | copy-start | bytes 884740
  0.7 12.7 %copy-start.9 = (s32[32]{0:T(128)S(1)}, s32[32]{0:T(128)}, u32[]{:S(2)}) copy-start(s32[32]{0:T(128)} %counts_ref.9) | copy-start | bytes 388
  0.7 14.3 %copy-start = (bf16[1536,3,128]{2,0,1:T(8,128)(2,1)S(1)}, bf16[1536,3,128]{2,0,1:T(8,128)(2,1)}, u32[]{:S(2)}) copy-start(bf16[1536,3,128]{2,0,1:T(8,128)(2,1)} %param.9) | copy-start | bytes 3538948
  0.7 14.3 %copy-start.1 = (bf16[128,1536]{1,0:T(8,128)(2,1)S(1)}, bf16[128,1536]{1,0:T(8,128)(2,1)}, u32[]{:S(2)}) copy-start(bf16[128,1536]{1,0:T(8,128)(2,1)} %w_out_ref.2) | copy-start | bytes 1179652
  4.2 14.4 %all-to-all-start = ((bf16[4,128,256]{2,1,0:T(8,128)(2,1)}), bf16[4,128,256]{2,1,0:T(8,128)(2,1)S(1)}, u32[]{:S(2)}, u32[]{:S(2)}) async-start(bf16[4,128,256]{2,1,0:T(8,128)(2,1)} %get-tuple-element.34), calls=%async_computation | async-start | bytes 524288 | tf_op jit(solution)/shard_map/all_to_all | solution.py:795
  14.2 0.8 %copy-start.5 = (f32[4,16,1536]{2,1,0:T(8,128)}, f32[4,16,1536]{2,1,0:T(8,128)S(1)}, u32[]{:S(2)}) copy-start(f32[4,16,1536]{2,1,0:T(8,128)S(1)} %get-tuple-element.44.factors_ref) | copy-start | bytes 1179652
  15.0 0.8 %copy-start.8 = (bf16[2,64,128]{2,1,0:T(8,128)(2,1)S(1)}, bf16[2,64,128]{2,1,0:T(8,128)(2,1)}, u32[]{:S(2)}) copy-start(bf16[2,64,128]{2,1,0:T(8,128)(2,1)} %get-tuple-element.42.raw_ref) | copy-start | bytes 98308
  18.6 16.3 %collective-permute-start.2 = (bf16[512,256]{1,0:T(8,128)(2,1)S(1)}, bf16[512,256]{1,0:T(8,128)(2,1)S(1)}, u32[]{:S(2)}, u32[]{:S(2)}) collective-permute-start(bf16[512,256]{1,0:T(8,128)(2,1)S(1)} %bitcast.6), channel_id=1, source_target_pairs={{0,32},{64,96},{128,160},{192,224},{256,288},{320,352},{384,416},{... | collective-permute-start | bytes 786440 | tf_op jit(solution)/shard_map/ppermute | solution.py:801
  20.5 15.5 %collective-permute-start.1 = (bf16[512,256]{1,0:T(8,128)(2,1)S(1)}, bf16[512,256]{1,0:T(8,128)(2,1)S(1)}, u32[]{:S(2)}, u32[]{:S(2)}) collective-permute-start(bf16[512,256]{1,0:T(8,128)(2,1)S(1)} %bitcast.7), channel_id=1, source_target_pairs={{480,0},{32,64},{96,128},{160,192},{224,256},{288,320},{352,384},{... | collective-permute-start | bytes 786440 | tf_op jit(solution)/shard_map/ppermute | solution.py:801
  28.7 11.4 %collective-permute-start = (bf16[256,256]{1,0:T(8,128)(2,1)S(1)}, bf16[256,256]{1,0:T(8,128)(2,1)S(1)}, u32[]{:S(2)}, u32[]{:S(2)}) collective-permute-start(bf16[256,256]{1,0:T(8,128)(2,1)S(1)} %bitcast.11), channel_id=1, source_target_pairs={{464,0},{449,1},{64,16},{81,17},{480,32},{497,33},{112,48},{97,49}... | collective-permute-start | bytes 393224 | tf_op jit(solution)/shard_map/ppermute | solution.py:814
  33.0 16.5 %collective-permute-start.3 = (bf16[6272,128]{1,0:T(8,128)(2,1)S(1)}, bf16[6272,128]{1,0:T(8,128)(2,1)S(1)}, u32[]{:S(2)}, u32[]{:S(2)}) collective-permute-start(bf16[6272,128]{1,0:T(8,128)(2,1)S(1)} %shard_map.88.weights_ref), channel_id=1, source_target_pairs={{0,1},{1,0},{2,3},{3,2},{4,5},{5,4},{6,7},{7,6},{8,9},{9,8},{10,11... | collective-permute-start | bytes 4816904 | tf_op jit(solution)/shard_map/ppermute | solution.py:819
  40.1 9.4 %copy-start.7 = (bf16[2,64,128]{2,1,0:T(8,128)(2,1)S(1)}, bf16[2,64,128]{2,1,0:T(8,128)(2,1)}, u32[]{:S(2)}) copy-start(bf16[2,64,128]{2,1,0:T(8,128)(2,1)} %get-tuple-element.64.raw_ref) | copy-start | bytes 98308
  40.1 9.4 %copy-start.10 = (f32[2,64]{1,0:T(2,128)S(1)}, f32[2,64]{1,0:T(2,128)}, u32[]{:S(2)}) copy-start(f32[2,64]{1,0:T(2,128)} %gains_ref.3) | copy-start | bytes 1540
  49.4 13.4 %copy-start.6 = (f32[4,16,1536]{2,1,0:T(8,128)S(1)}, f32[4,16,1536]{2,1,0:T(8,128)}, u32[]{:S(2)}) copy-start(f32[4,16,1536]{2,1,0:T(8,128)} %copy-done.5) | copy-start | bytes 1179652

commit v4 on v2

--- a/solution.py
+++ b/solution.py
@@ -307,7 +307,7 @@
 ):
     half, _, starts, ends, _, _ = window_facts(counts_ref)
     block_rows = CHUNK // 2
-    to_first = jnp.where(lax.rem(lax.axis_index("z"), 2) == 0, 2 * CHUNK, -2 * CHUNK)
+    to_first = jnp.where(lax.rem(lax.axis_index("z"), 2) == 1, 2 * CHUNK, -2 * CHUNK)
     for block in range(8):
         at = slice(block * block_rows, (block + 1) * block_rows)
         inner = slice(block % 4 * block_rows, (block % 4 + 1) * block_rows)
@@ -373,9 +373,9 @@
 ):
     half, own_at, starts, ends, left_from, right_to = window_facts(counts_ref)
     block_rows = CHUNK // 2
-    even = lax.rem(lax.axis_index("z"), 2) == 0
-    first_at = pl.multiple_of(jnp.where(even, 4 * CHUNK, 0), 2 * CHUNK)
-    second_at = pl.multiple_of(jnp.where(even, 0, 4 * CHUNK), 2 * CHUNK)
+    odd = lax.rem(lax.axis_index("z"), 2) == 1
+    first_at = pl.multiple_of(jnp.where(odd, 4 * CHUNK, 0), 2 * CHUNK)
+    second_at = pl.multiple_of(jnp.where(odd, 0, 4 * CHUNK), 2 * CHUNK)
     early = ((qa_ref, qx_ref), (ka_ref, kx_ref), (va_ref, vx_ref), (da_ref, dx_ref))
     for source, target in early:
         target[2 * CHUNK : 4 * CHUNK, :] = source[0 : 2 * CHUNK, :]
@@ -796,7 +796,7 @@
     mine, rows, factors, weights = lax.optimization_barrier((mine, rows, factors, weights))
     mine = mine.reshape(quad * tok_rows, 2 * LANES)
     evens = range(0, z_count, 2)
-    swaps = [(i, i + 1) for i in evens], [((i - 1) % z_count, i) for i in evens]
+    swaps = [((i - 1) % z_count, i) for i in evens], [(i, i + 1) for i in evens]
     first, second = (
         lax.ppermute(mine, "z", pairs + [(j, i) for i, j in pairs]) for pairs in swaps
     )

time: 62.3 us -> 64.1 us (1.029)
  waiting for transfers between devices: 3.71 us -> 6 us
  starting transfers between devices: 23.1 us -> 22.2 us
    ppermute x2, waiting for transfers between devices: 1.66 us -> 3.95 us  [per_device(): lax.ppermute(mine, 'z', pairs + [(j, i) for i, j in pairs])]
    ppermute x2, starting transfers between devices: 10 us -> 9.02 us  [per_device(): lax.ppermute(mine, 'z', pairs + [(j, i) for i, j in pairs])]
where the time goes in v4:
time: 64.1 us; the launch traced here: 63.6 us
  starting transfers between devices  22.2 us (35%)
  blocking collectives  19 us (30%)
  Pallas kernels  14 us (22%)
  waiting for transfers between devices  6 us (9%)
  local copies, waits for them, and re-layouts  1.55 us (2%)
  between operations  0.83 us (1%)
    all_to_all x1, blocking collectives, per_device(): shares = lax.all_to_all(partial, 'x', 0, 0)  12.2 us
    all_to_all x1, starting transfers between devices, per_device(): mine = lax.all_to_all(heads, ('yh', 'yl'), 0, 0)  9.19 us
    ppermute x2, starting transfers between devices, per_device(): lax.ppermute(mine, 'z', pairs + [(j, i) for i, j in pairs])  9.02 us
    all_to_all x1, blocking collectives, per_device(): parts = lax.all_to_all(parts, ('yl', 'core'), 0, 0)  6.79 us
    ppermute x2, waiting for transfers between devices, per_device(): lax.ppermute(mine, 'z', pairs + [(j, i) for i, j in pairs])  3.95 us
    pallas_call x1, Pallas kernels, enter(): pl.pallas_call(enter_kernel, out_shape=(jax.ShapeDtypeStruct((quad, rows,...  3.51 us
    pallas_call x1, Pallas kernels, attend_near(): pl.pallas_call(near_kernel, out_shape=(head_rows,) * 4 + (jax.ShapeDtypeS...  3.25 us
    pallas_call x1, Pallas kernels, attend_far(): pl.pallas_call(far_kernel, out_shape=jax.ShapeDtypeStruct((4, CHUNK // 4,...  2.52 us
  transfers between devices with their start and end apart: 5, of which 2 were waited for; matrix products, arithmetic and copies ran while one was open for 0% of the time, Pallas kernels for 13%

profile of v4, /device:TPU:8, one launch (start us, length us, event | category | flops | bytes accessed | tf_op | source)
XLA Modules:
  0.0 63.6 jit_solution(12052413330348620052)
XLA Ops:
  0.6 0.0 copy-start.2
  0.6 0.0 copy-start.3
  0.7 0.0 copy-start.4
  0.7 0.0 copy-start.9
  0.7 0.0 copy-start
  0.7 0.0 copy-start.1
  0.7 3.5 %shard_map.86 = (bf16[4,128,256]{2,1,0:T(8,128)(2,1)}, bf16[2,64,128]{2,1,0:T(8,128)(2,1)}, bf16[2,64,128]{2,1,0:T(8,128)(2,1)}) custom-call(s32[32]{0:T(128)} %counts_ref.9, f32[2,64]{1,0:T(2,128)} %gains_ref.3, bf16[128,1536]{1,0:T(8,128)(2,1)} %tokens_ref.2, bf16[128,1536]{1,0:T(8,128)(2,1)} %cotangent_ref.2, bf16[3,1536,128]{2,1,0:T(8,128)(2,1)} %bitcast.4, ...), custom_call_target="tpu_custom_call" | custom-call | tf_op jit(solution)/shard_map/pallas_call | solution.py:144
  4.2 9.2 %all-to-all-start = ((bf16[4,128,256]{2,1,0:T(8,128)(2,1)}), bf16[4,128,256]{2,1,0:T(8,128)(2,1)S(1)}, u32[]{:S(2)}, u32[]{:S(2)}) async-start(bf16[4,128,256]{2,1,0:T(8,128)(2,1)} %get-tuple-element.34), calls=%async_computation | async-start | bytes 524288 | tf_op jit(solution)/shard_map/all_to_all | solution.py:795
  13.4 0.0 copy-done.2
  13.4 0.0 copy-done.3
  13.4 0.0 copy-done.4
  13.4 0.0 copy-done.9
  13.4 0.8 %shard_map.87 = (bf16[2,16,1536]{2,1,0:T(8,128)(2,1)S(1)}, f32[4,16,1536]{2,1,0:T(8,128)S(1)}) custom-call(s32[32]{0:T(128)S(1)} %copy-done.9, bf16[128,1536]{1,0:T(8,128)(2,1)S(1)} %copy-done.2, bf16[128,1536]{1,0:T(8,128)(2,1)S(1)} %copy-done.3, bf16[3,32,1536]{2,1,0:T(8,128)(2,1)S(1)} %bitcast.10), custom_call_target="tpu_custom_call" | custom-call | tf_op jit(solution)/shard_map/pallas_call | solution.py:737
  14.2 0.0 copy-start.5
  14.2 0.7 %copy-done.5 = f32[4,16,1536]{2,1,0:T(8,128)} copy-done((f32[4,16,1536]{2,1,0:T(8,128)}, f32[4,16,1536]{2,1,0:T(8,128)S(1)}, u32[]{:S(2)}) %copy-start.5) | copy-done | bytes 393240
  14.9 0.0 copy-done
  15.0 0.0 copy-done.1
  15.0 0.0 copy-start.8
  15.0 0.8 %copy-done.8 = bf16[2,64,128]{2,1,0:T(8,128)(2,1)S(1)} copy-done((bf16[2,64,128]{2,1,0:T(8,128)(2,1)S(1)}, bf16[2,64,128]{2,1,0:T(8,128)(2,1)}, u32[]{:S(2)}) %copy-start.8) | copy-done | bytes 32792
  15.7 0.9 %shard_map.88.weights_ref = bf16[6272,128]{1,0:T(8,128)(2,1)S(1)} custom-call(bf16[3,1536,128]{2,1,0:T(8,128)(2,1)S(1)} %bitcast.5, bf16[128,1536]{1,0:T(8,128)(2,1)S(1)} %copy-done.1, bf16[2,64,128]{2,1,0:T(8,128)(2,1)S(1)} %copy-done.8), custom_call_target="tpu_custom_call" | custom-call | tf_op jit(solution)/shard_map/pallas_call | solution.py:185
  16.6 2.0 %all-to-all-done = bf16[4,128,256]{2,1,0:T(8,128)(2,1)S(1)} async-done(((bf16[4,128,256]{2,1,0:T(8,128)(2,1)}), bf16[4,128,256]{2,1,0:T(8,128)(2,1)S(1)}, u32[]{:S(2)}, u32[]{:S(2)}) %all-to-all-start) | async-done | bytes 262176 | tf_op jit(solution)/shard_map/all_to_all | solution.py:795
  18.6 7.1 %collective-permute-start.2 = (bf16[512,256]{1,0:T(8,128)(2,1)S(1)}, bf16[512,256]{1,0:T(8,128)(2,1)S(1)}, u32[]{:S(2)}, u32[]{:S(2)}) collective-permute-start(bf16[512,256]{1,0:T(8,128)(2,1)S(1)} %bitcast.6), channel_id=1, source_target_pairs={{480,0},{32,64},{96,128},{160,192},{224,256},{288,320},{352,384},{... | collective-permute-start | bytes 786440 | tf_op jit(solution)/shard_map/ppermute | solution.py:801
  25.7 1.9 %collective-permute-start.1 = (bf16[512,256]{1,0:T(8,128)(2,1)S(1)}, bf16[512,256]{1,0:T(8,128)(2,1)S(1)}, u32[]{:S(2)}, u32[]{:S(2)}) collective-permute-start(bf16[512,256]{1,0:T(8,128)(2,1)S(1)} %bitcast.7), channel_id=1, source_target_pairs={{0,32},{64,96},{128,160},{192,224},{256,288},{320,352},{384,416},{... | collective-permute-start | bytes 786440 | tf_op jit(solution)/shard_map/ppermute | solution.py:801
  27.7 1.9 %collective-permute-start = (bf16[256,256]{1,0:T(8,128)(2,1)S(1)}, bf16[256,256]{1,0:T(8,128)(2,1)S(1)}, u32[]{:S(2)}, u32[]{:S(2)}) collective-permute-start(bf16[256,256]{1,0:T(8,128)(2,1)S(1)} %bitcast.11), channel_id=1, source_target_pairs={{448,0},{465,1},{80,16},{65,17},{480,32},{497,33},{112,48},{97,49}... | collective-permute-start | bytes 393224 | tf_op jit(solution)/shard_map/ppermute | solution.py:812
  29.6 2.1 %collective-permute-start.3 = (bf16[6272,128]{1,0:T(8,128)(2,1)S(1)}, bf16[6272,128]{1,0:T(8,128)(2,1)S(1)}, u32[]{:S(2)}, u32[]{:S(2)}) collective-permute-start(bf16[6272,128]{1,0:T(8,128)(2,1)S(1)} %shard_map.88.weights_ref), channel_id=1, source_target_pairs={{0,1},{1,0},{2,3},{3,2},{4,5},{5,4},{6,7},{7,6},{8,9},{9,8},{10,11... | collective-permute-start | bytes 4816904 | tf_op jit(solution)/shard_map/ppermute | solution.py:817
  31.7 0.0 collective-permute-done.2.first_ref
  31.7 1.1 %shard_map.89 = (bf16[1024,128]{1,0:T(8,128)(2,1)S(1)}, bf16[1024,128]{1,0:T(8,128)(2,1)S(1)}, bf16[1024,128]{1,0:T(8,128)(2,1)S(1)}, bf16[1024,128]{1,0:T(8,128...) custom-call(s32[32]{0:T(128)S(1)} %copy-done.9, ...), custom_call_target="tpu_custom_call" | custom-call | tf_op jit(solution)/shard_map/pallas_call | solution.py:339
  32.9 3.9 %collective-permute-done.1.second_ref = bf16[512,256]{1,0:T(8,128)(2,1)S(1)} collective-permute-done((bf16[512,256]{1,0:T(8,128)(2,1)S(1)}, bf16[512,256]{1,0:T(8,128)(2,1)S(1)}, u32[]{:S(2)}, u32[]{:S(2)}) %collective-permute-start.1) | collective-permute-done | bytes 262176 | tf_op jit(solution)/shard_map/ppermute | solution.py:801
  36.8 3.2 %shard_map.90 = (bf16[1536,128]{1,0:T(8,128)(2,1)S(1)}, bf16[1536,128]{1,0:T(8,128)(2,1)S(1)}, bf16[1536,128]{1,0:T(8,128)(2,1)S(1)}, bf16[1536,128]{1,0:T(8,128...) custom-call(s32[32]{0:T(128)S(1)} %copy-done.9, ...), custom_call_target="tpu_custom_call" | custom-call | flops 8999999488 | bytes 1048576 | tf_op jit(solution)/shard_map/pallas_call | solution.py:460
  40.1 0.0 collective-permute-done.far_ref
  40.1 0.0 copy-start.7
  40.1 0.0 copy-start.10
  40.1 2.5 %shard_map.91 = bf16[4,64,256]{2,1,0:T(8,128)(2,1)S(1)} custom-call(s32[32]{0:T(128)S(1)} %copy-done.9, bf16[256,256]{1,0:T(8,128)(2,1)S(1)} %collective-permute-done.far_ref, bf16[1536,128]{1,0:T(8,128)(2,1)S(1)} %get-tuple-element.54.qx_ref, bf16[1536,128]{1,0:T(8,128)(2,1)S(1)} %get-tuple-element.55.kx_ref, ...), custom_call_target="tpu_custom_call" | custom-call | flops 8999999488 | bytes 1048576 | tf_op jit(solution)/shard_map/pallas_call | solution.py:634
  42.6 6.8 %all_to_all.15.parts_ref = bf16[4,64,256]{2,1,0:T(8,128)(2,1)S(1)} all-to-all(bf16[4,64,256]{2,1,0:T(8,128)(2,1)S(1)} %shard_map.91), channel_id=1, replica_groups=mesh['z'=16,'yh'=2,'yl'=2,'x'=4,'core'=2] {'yl','core'}, dimensions={0} | all-to-all | bytes 262144 | tf_op jit(solution)/shard_map/all_to_all | solution.py:819
  49.4 0.0 collective-permute-done.3.weights_far_ref
  49.4 0.0 copy-done.7
  49.4 0.0 copy-done.10
  49.4 0.0 copy-start.6
  49.5 1.2 %shard_map.92 = bf16[4,16,3072]{2,1,0:T(8,128)(2,1)S(1)} custom-call(bf16[4,64,256]{2,1,0:T(8,128)(2,1)S(1)} %all_to_all.15.parts_ref, f32[2,64]{1,0:T(2,128)S(1)} %copy-done.10, bf16[2,64,128]{2,1,0:T(8,128)(2,1)S(1)} %copy-done.7, bf16[6272,128]{1,0:T(8,128)(2,1)S(1)} %shard_map.88.weights_ref, bf16[6272,128]{1,0:T(8,128)(2,1)S(1)} %collective-permute-done.3.weights_far_ref), custom_call_target="tpu_custom_call" | custom-call | tf_op jit(solution)/shard_map/pallas_call | solution.py:704
  50.6 12.2 %all_to_all.16.shares_ref = bf16[4,16,3072]{2,1,0:T(8,128)(2,1)S(1)} all-to-all(bf16[4,16,3072]{2,1,0:T(8,128)(2,1)S(1)} %shard_map.92), channel_id=1, replica_groups=mesh['z'=16,'yh'=2,'yl'=2,'x'=4,'core'=2] {'x'}, dimensions={0} | all-to-all | bytes 786432 | tf_op jit(solution)/shard_map/all_to_all | solution.py:821
  62.9 0.0 copy-done.6
  62.9 0.7 %shard_map.93 = (bf16[16,1536]{1,0:T(8,128)(2,1)}, bf16[16,1536]{1,0:T(8,128)(2,1)}) custom-call(bf16[2,16,1536]{2,1,0:T(8,128)(2,1)S(1)} %get-tuple-element.43.rows_ref, f32[4,16,1536]{2,1,0:T(8,128)S(1)} %copy-done.6, bf16[4,16,3072]{2,1,0:T(8,128)(2,1)S(1)} %all_to_all.16.shares_ref), custom_call_target="tpu_custom_call" | custom-call | tf_op jit(solution)/shard_map/pallas_call | solution.py:768
  (1 shorter events, 0.0 us)
Async XLA Ops:
  0.6 12.8 %copy-start.2 = (bf16[128,1536]{1,0:T(8,128)(2,1)S(1)}, bf16[128,1536]{1,0:T(8,128)(2,1)}, u32[]{:S(2)}) copy-start(bf16[128,1536]{1,0:T(8,128)(2,1)} %tokens_ref.2) | copy-start | bytes 1179652
  0.6 12.8 %copy-start.3 = (bf16[128,1536]{1,0:T(8,128)(2,1)S(1)}, bf16[128,1536]{1,0:T(8,128)(2,1)}, u32[]{:S(2)}) copy-start(bf16[128,1536]{1,0:T(8,128)(2,1)} %cotangent_ref.2) | copy-start | bytes 1179652
  0.7 12.8 %copy-start.4 = (bf16[32,3,1536]{2,0,1:T(8,128)(2,1)S(1)}, bf16[32,3,1536]{2,0,1:T(8,128)(2,1)}, u32[]{:S(2)}) copy-start(bf16[32,3,1536]{2,0,1:T(8,128)(2,1)} %param.12) | copy-start | bytes 884740
  0.7 12.7 %copy-start.9 = (s32[32]{0:T(128)S(1)}, s32[32]{0:T(128)}, u32[]{:S(2)}) copy-start(s32[32]{0:T(128)} %counts_ref.9) | copy-start | bytes 388
  0.7 14.3 %copy-start = (bf16[1536,3,128]{2,0,1:T(8,128)(2,1)S(1)}, bf16[1536,3,128]{2,0,1:T(8,128)(2,1)}, u32[]{:S(2)}) copy-start(bf16[1536,3,128]{2,0,1:T(8,128)(2,1)} %param.9) | copy-start | bytes 3538948
  0.7 14.3 %copy-start.1 = (bf16[128,1536]{1,0:T(8,128)(2,1)S(1)}, bf16[128,1536]{1,0:T(8,128)(2,1)}, u32[]{:S(2)}) copy-start(bf16[128,1536]{1,0:T(8,128)(2,1)} %w_out_ref.2) | copy-start | bytes 1179652
  4.2 14.4 %all-to-all-start = ((bf16[4,128,256]{2,1,0:T(8,128)(2,1)}), bf16[4,128,256]{2,1,0:T(8,128)(2,1)S(1)}, u32[]{:S(2)}, u32[]{:S(2)}) async-start(bf16[4,128,256]{2,1,0:T(8,128)(2,1)} %get-tuple-element.34), calls=%async_computation | async-start | bytes 524288 | tf_op jit(solution)/shard_map/all_to_all | solution.py:795
  14.2 0.8 %copy-start.5 = (f32[4,16,1536]{2,1,0:T(8,128)}, f32[4,16,1536]{2,1,0:T(8,128)S(1)}, u32[]{:S(2)}) copy-start(f32[4,16,1536]{2,1,0:T(8,128)S(1)} %get-tuple-element.44.factors_ref) | copy-start | bytes 1179652
  15.0 0.8 %copy-start.8 = (bf16[2,64,128]{2,1,0:T(8,128)(2,1)S(1)}, bf16[2,64,128]{2,1,0:T(8,128)(2,1)}, u32[]{:S(2)}) copy-start(bf16[2,64,128]{2,1,0:T(8,128)(2,1)} %get-tuple-element.42.raw_ref) | copy-start | bytes 98308
  18.6 13.1 %collective-permute-start.2 = (bf16[512,256]{1,0:T(8,128)(2,1)S(1)}, bf16[512,256]{1,0:T(8,128)(2,1)S(1)}, u32[]{:S(2)}, u32[]{:S(2)}) collective-permute-start(bf16[512,256]{1,0:T(8,128)(2,1)S(1)} %bitcast.6), channel_id=1, source_target_pairs={{480,0},{32,64},{96,128},{160,192},{224,256},{288,320},{352,384},{... | collective-permute-start | bytes 786440 | tf_op jit(solution)/shard_map/ppermute | solution.py:801
  25.7 11.1 %collective-permute-start.1 = (bf16[512,256]{1,0:T(8,128)(2,1)S(1)}, bf16[512,256]{1,0:T(8,128)(2,1)S(1)}, u32[]{:S(2)}, u32[]{:S(2)}) collective-permute-start(bf16[512,256]{1,0:T(8,128)(2,1)S(1)} %bitcast.7), channel_id=1, source_target_pairs={{0,32},{64,96},{128,160},{192,224},{256,288},{320,352},{384,416},{... | collective-permute-start | bytes 786440 | tf_op jit(solution)/shard_map/ppermute | solution.py:801
  27.7 12.4 %collective-permute-start = (bf16[256,256]{1,0:T(8,128)(2,1)S(1)}, bf16[256,256]{1,0:T(8,128)(2,1)S(1)}, u32[]{:S(2)}, u32[]{:S(2)}) collective-permute-start(bf16[256,256]{1,0:T(8,128)(2,1)S(1)} %bitcast.11), channel_id=1, source_target_pairs={{448,0},{465,1},{80,16},{65,17},{480,32},{497,33},{112,48},{97,49}... | collective-permute-start | bytes 393224 | tf_op jit(solution)/shard_map/ppermute | solution.py:812
  29.6 19.8 %collective-permute-start.3 = (bf16[6272,128]{1,0:T(8,128)(2,1)S(1)}, bf16[6272,128]{1,0:T(8,128)(2,1)S(1)}, u32[]{:S(2)}, u32[]{:S(2)}) collective-permute-start(bf16[6272,128]{1,0:T(8,128)(2,1)S(1)} %shard_map.88.weights_ref), channel_id=1, source_target_pairs={{0,1},{1,0},{2,3},{3,2},{4,5},{5,4},{6,7},{7,6},{8,9},{9,8},{10,11... | collective-permute-start | bytes 4816904 | tf_op jit(solution)/shard_map/ppermute | solution.py:817
  40.1 9.3 %copy-start.7 = (bf16[2,64,128]{2,1,0:T(8,128)(2,1)S(1)}, bf16[2,64,128]{2,1,0:T(8,128)(2,1)}, u32[]{:S(2)}) copy-start(bf16[2,64,128]{2,1,0:T(8,128)(2,1)} %get-tuple-element.64.raw_ref) | copy-start | bytes 98308
  40.1 9.3 %copy-start.10 = (f32[2,64]{1,0:T(2,128)S(1)}, f32[2,64]{1,0:T(2,128)}, u32[]{:S(2)}) copy-start(f32[2,64]{1,0:T(2,128)} %gains_ref.3) | copy-start | bytes 1540
  49.4 13.4 %copy-start.6 = (f32[4,16,1536]{2,1,0:T(8,128)S(1)}, f32[4,16,1536]{2,1,0:T(8,128)}, u32[]{:S(2)}) copy-start(f32[4,16,1536]{2,1,0:T(8,128)} %copy-done.5) | copy-start | bytes 1179652

commit v5 on v2

--- a/solution.py
+++ b/solution.py
@@ -813,8 +813,10 @@
         far_half, ("z", "yh", "core"), [(far_source(i), i) for i in range(halves)]
     )
     early = attend_early(image_counts, first, mine)
+    weights_late, early_first = lax.optimization_barrier((weights, early[0]))
+    early = (early_first,) + tuple(early[1:])
     near_parts = attend_near(image_counts, second, early)
-    weights_far = lax.ppermute(weights, "core", [(0, 1), (1, 0)])
+    weights_far = lax.ppermute(weights_late, "core", [(0, 1), (1, 0)])
     parts = attend_far(image_counts, far, near_parts)
     parts = lax.all_to_all(parts, ("yl", "core"), 0, 0)
     partial = project(parts, qk_gain, raw, weights, weights_far, x_count, model_width)

time: 62.3 us -> 62.3 us (level)
  no operation moved by 1% of the time
where the time goes in v5:
time: 62.3 us; the launch traced here: 61.6 us
  starting transfers between devices  23.1 us (37%)
  blocking collectives  19 us (30%)
  Pallas kernels  13.4 us (22%)
  waiting for transfers between devices  3.71 us (6%)
  local copies, waits for them, and re-layouts  1.55 us (2%)
  between operations  0.83 us (1%)
    all_to_all x1, blocking collectives, per_device(): shares = lax.all_to_all(partial, 'x', 0, 0)  12.2 us
    ppermute x2, starting transfers between devices, per_device(): lax.ppermute(mine, 'z', pairs + [(j, i) for i, j in pairs])  10 us
    all_to_all x1, starting transfers between devices, per_device(): mine = lax.all_to_all(heads, ('yh', 'yl'), 0, 0)  9.19 us
    all_to_all x1, blocking collectives, per_device(): parts = lax.all_to_all(parts, ('yl', 'core'), 0, 0)  6.79 us
    pallas_call x1, Pallas kernels, enter(): pl.pallas_call(enter_kernel, out_shape=(jax.ShapeDtypeStruct((quad, rows,...  3.51 us
    pallas_call x1, Pallas kernels, attend_near(): pl.pallas_call(near_kernel, out_shape=(head_rows,) * 4 + (jax.ShapeDtypeS...  2.72 us
    pallas_call x1, Pallas kernels, attend_far(): pl.pallas_call(far_kernel, out_shape=jax.ShapeDtypeStruct((4, CHUNK // 4,...  2.52 us
    all_to_all x1, waiting for transfers between devices, per_device(): mine = lax.all_to_all(heads, ('yh', 'yl'), 0, 0)  2.05 us
  transfers between devices with their start and end apart: 5, of which 2 were waited for; matrix products, arithmetic and copies ran while one was open for 0% of the time, Pallas kernels for 13%

profile of v5, /device:TPU:8, one launch (start us, length us, event | category | flops | bytes accessed | tf_op | source)
XLA Modules:
  0.0 61.6 jit_solution(11820635970628687673)
XLA Ops:
  0.6 0.0 copy-start.2
  0.6 0.0 copy-start.3
  0.7 0.0 copy-start.4
  0.7 0.0 copy-start.9
  0.7 0.0 copy-start
  0.7 0.0 copy-start.1
  0.7 3.5 %shard_map.86 = (bf16[4,128,256]{2,1,0:T(8,128)(2,1)}, bf16[2,64,128]{2,1,0:T(8,128)(2,1)}, bf16[2,64,128]{2,1,0:T(8,128)(2,1)}) custom-call(s32[32]{0:T(128)} %counts_ref.9, f32[2,64]{1,0:T(2,128)} %gains_ref.3, bf16[128,1536]{1,0:T(8,128)(2,1)} %tokens_ref.2, bf16[128,1536]{1,0:T(8,128)(2,1)} %cotangent_ref.2, bf16[3,1536,128]{2,1,0:T(8,128)(2,1)} %bitcast.4, ...), custom_call_target="tpu_custom_call" | custom-call | tf_op jit(solution)/shard_map/pallas_call | solution.py:144
  4.2 9.2 %all-to-all-start = ((bf16[4,128,256]{2,1,0:T(8,128)(2,1)}), bf16[4,128,256]{2,1,0:T(8,128)(2,1)S(1)}, u32[]{:S(2)}, u32[]{:S(2)}) async-start(bf16[4,128,256]{2,1,0:T(8,128)(2,1)} %get-tuple-element.36), calls=%async_computation | async-start | bytes 524288 | tf_op jit(solution)/shard_map/all_to_all | solution.py:795
  13.4 0.0 copy-done.2
  13.4 0.0 copy-done.3
  13.4 0.0 copy-done.4
  13.4 0.0 copy-done.9
  13.4 0.8 %shard_map.87 = (bf16[2,16,1536]{2,1,0:T(8,128)(2,1)S(1)}, f32[4,16,1536]{2,1,0:T(8,128)S(1)}) custom-call(s32[32]{0:T(128)S(1)} %copy-done.9, bf16[128,1536]{1,0:T(8,128)(2,1)S(1)} %copy-done.2, bf16[128,1536]{1,0:T(8,128)(2,1)S(1)} %copy-done.3, bf16[3,32,1536]{2,1,0:T(8,128)(2,1)S(1)} %bitcast.10), custom_call_target="tpu_custom_call" | custom-call | tf_op jit(solution)/shard_map/pallas_call | solution.py:737
  14.2 0.0 copy-start.5
  14.2 0.7 %copy-done.5 = f32[4,16,1536]{2,1,0:T(8,128)} copy-done((f32[4,16,1536]{2,1,0:T(8,128)}, f32[4,16,1536]{2,1,0:T(8,128)S(1)}, u32[]{:S(2)}) %copy-start.5) | copy-done | bytes 393240
  14.9 0.0 copy-done
  15.0 0.0 copy-done.1
  15.0 0.0 copy-start.8
  15.0 0.8 %copy-done.8 = bf16[2,64,128]{2,1,0:T(8,128)(2,1)S(1)} copy-done((bf16[2,64,128]{2,1,0:T(8,128)(2,1)S(1)}, bf16[2,64,128]{2,1,0:T(8,128)(2,1)}, u32[]{:S(2)}) %copy-start.8) | copy-done | bytes 32792
  15.7 0.9 %shard_map.88.weights_ref = bf16[6272,128]{1,0:T(8,128)(2,1)S(1)} custom-call(bf16[3,1536,128]{2,1,0:T(8,128)(2,1)S(1)} %bitcast.5, bf16[128,1536]{1,0:T(8,128)(2,1)S(1)} %copy-done.1, bf16[2,64,128]{2,1,0:T(8,128)(2,1)S(1)} %copy-done.8), custom_call_target="tpu_custom_call" | custom-call | tf_op jit(solution)/shard_map/pallas_call | solution.py:185
  16.6 2.0 %all-to-all-done = bf16[4,128,256]{2,1,0:T(8,128)(2,1)S(1)} async-done(((bf16[4,128,256]{2,1,0:T(8,128)(2,1)}), bf16[4,128,256]{2,1,0:T(8,128)(2,1)S(1)}, u32[]{:S(2)}, u32[]{:S(2)}) %all-to-all-start) | async-done | bytes 262176 | tf_op jit(solution)/shard_map/all_to_all | solution.py:795
  18.6 1.9 %collective-permute-start.2 = (bf16[512,256]{1,0:T(8,128)(2,1)S(1)}, bf16[512,256]{1,0:T(8,128)(2,1)S(1)}, u32[]{:S(2)}, u32[]{:S(2)}) collective-permute-start(bf16[512,256]{1,0:T(8,128)(2,1)S(1)} %bitcast.6), channel_id=1, source_target_pairs={{0,32},{64,96},{128,160},{192,224},{256,288},{320,352},{384,416},{... | collective-permute-start | bytes 786440 | tf_op jit(solution)/shard_map/ppermute | solution.py:801
  20.5 8.1 %collective-permute-start.1 = (bf16[512,256]{1,0:T(8,128)(2,1)S(1)}, bf16[512,256]{1,0:T(8,128)(2,1)S(1)}, u32[]{:S(2)}, u32[]{:S(2)}) collective-permute-start(bf16[512,256]{1,0:T(8,128)(2,1)S(1)} %bitcast.7), channel_id=1, source_target_pairs={{480,0},{32,64},{96,128},{160,192},{224,256},{288,320},{352,384},{... | collective-permute-start | bytes 786440 | tf_op jit(solution)/shard_map/ppermute | solution.py:801
  28.7 1.9 %collective-permute-start = (bf16[256,256]{1,0:T(8,128)(2,1)S(1)}, bf16[256,256]{1,0:T(8,128)(2,1)S(1)}, u32[]{:S(2)}, u32[]{:S(2)}) collective-permute-start(bf16[256,256]{1,0:T(8,128)(2,1)S(1)} %bitcast.11), channel_id=1, source_target_pairs={{448,0},{465,1},{80,16},{65,17},{480,32},{497,33},{112,48},{97,49}... | collective-permute-start | bytes 393224 | tf_op jit(solution)/shard_map/ppermute | solution.py:812
  30.6 0.0 collective-permute-done.2.first_ref
  30.6 1.1 %shard_map.89 = (bf16[1024,128]{1,0:T(8,128)(2,1)S(1)}, bf16[1024,128]{1,0:T(8,128)(2,1)S(1)}, bf16[1024,128]{1,0:T(8,128)(2,1)S(1)}, bf16[1024,128]{1,0:T(8,128...) custom-call(s32[32]{0:T(128)S(1)} %copy-done.9, ...), custom_call_target="tpu_custom_call" | custom-call | tf_op jit(solution)/shard_map/pallas_call | solution.py:339
  31.8 1.9 %collective-permute-start.3 = (bf16[6272,128]{1,0:T(8,128)(2,1)S(1)}, bf16[6272,128]{1,0:T(8,128)(2,1)S(1)}, u32[]{:S(2)}, u32[]{:S(2)}) collective-permute-start(bf16[6272,128]{1,0:T(8,128)(2,1)S(1)} %shard_map.88.weights_ref), channel_id=1, source_target_pairs={{0,1},{1,0},{2,3},{3,2},{4,5},{5,4},{6,7},{7,6},{8,9},{9,8},{10,11... | collective-permute-start | bytes 4816904 | tf_op jit(solution)/shard_map/ppermute | solution.py:819
  33.7 1.7 %collective-permute-done.1.second_ref = bf16[512,256]{1,0:T(8,128)(2,1)S(1)} collective-permute-done((bf16[512,256]{1,0:T(8,128)(2,1)S(1)}, bf16[512,256]{1,0:T(8,128)(2,1)S(1)}, u32[]{:S(2)}, u32[]{:S(2)}) %collective-permute-start.1) | collective-permute-done | bytes 262176 | tf_op jit(solution)/shard_map/ppermute | solution.py:801
  35.4 2.7 %shard_map.90 = (bf16[1536,128]{1,0:T(8,128)(2,1)S(1)}, bf16[1536,128]{1,0:T(8,128)(2,1)S(1)}, bf16[1536,128]{1,0:T(8,128)(2,1)S(1)}, bf16[1536,128]{1,0:T(8,128...) custom-call(s32[32]{0:T(128)S(1)} %copy-done.9, ...), custom_call_target="tpu_custom_call" | custom-call | flops 8999999488 | bytes 1048576 | tf_op jit(solution)/shard_map/pallas_call | solution.py:460
  38.1 0.0 collective-permute-done.far_ref
  38.1 0.0 copy-start.7
  38.1 0.0 copy-start.10
  38.1 2.5 %shard_map.91 = bf16[4,64,256]{2,1,0:T(8,128)(2,1)S(1)} custom-call(s32[32]{0:T(128)S(1)} %copy-done.9, bf16[256,256]{1,0:T(8,128)(2,1)S(1)} %collective-permute-done.far_ref, bf16[1536,128]{1,0:T(8,128)(2,1)S(1)} %get-tuple-element.58.qx_ref, bf16[1536,128]{1,0:T(8,128)(2,1)S(1)} %get-tuple-element.59.kx_ref, ...), custom_call_target="tpu_custom_call" | custom-call | flops 8999999488 | bytes 1048576 | tf_op jit(solution)/shard_map/pallas_call | solution.py:634
  40.6 6.8 %all_to_all.15.parts_ref = bf16[4,64,256]{2,1,0:T(8,128)(2,1)S(1)} all-to-all(bf16[4,64,256]{2,1,0:T(8,128)(2,1)S(1)} %shard_map.91), channel_id=1, replica_groups=mesh['z'=16,'yh'=2,'yl'=2,'x'=4,'core'=2] {'yl','core'}, dimensions={0} | all-to-all | bytes 262144 | tf_op jit(solution)/shard_map/all_to_all | solution.py:821
  47.4 0.0 collective-permute-done.3.weights_far_ref
  47.4 0.0 copy-done.7
  47.4 0.0 copy-done.10
  47.4 0.0 copy-start.6
  47.4 1.2 %shard_map.92 = bf16[4,16,3072]{2,1,0:T(8,128)(2,1)S(1)} custom-call(bf16[4,64,256]{2,1,0:T(8,128)(2,1)S(1)} %all_to_all.15.parts_ref, f32[2,64]{1,0:T(2,128)S(1)} %copy-done.10, bf16[2,64,128]{2,1,0:T(8,128)(2,1)S(1)} %copy-done.7, bf16[6272,128]{1,0:T(8,128)(2,1)S(1)} %shard_map.88.weights_ref, bf16[6272,128]{1,0:T(8,128)(2,1)S(1)} %collective-permute-done.3.weights_far_ref), custom_call_target="tpu_custom_call" | custom-call | tf_op jit(solution)/shard_map/pallas_call | solution.py:704
  48.6 12.2 %all_to_all.16.shares_ref = bf16[4,16,3072]{2,1,0:T(8,128)(2,1)S(1)} all-to-all(bf16[4,16,3072]{2,1,0:T(8,128)(2,1)S(1)} %shard_map.92), channel_id=1, replica_groups=mesh['z'=16,'yh'=2,'yl'=2,'x'=4,'core'=2] {'x'}, dimensions={0} | all-to-all | bytes 786432 | tf_op jit(solution)/shard_map/all_to_all | solution.py:823
  60.9 0.0 copy-done.6
  60.9 0.7 %shard_map.93 = (bf16[16,1536]{1,0:T(8,128)(2,1)}, bf16[16,1536]{1,0:T(8,128)(2,1)}) custom-call(bf16[2,16,1536]{2,1,0:T(8,128)(2,1)S(1)} %get-tuple-element.45.rows_ref, f32[4,16,1536]{2,1,0:T(8,128)S(1)} %copy-done.6, bf16[4,16,3072]{2,1,0:T(8,128)(2,1)S(1)} %all_to_all.16.shares_ref), custom_call_target="tpu_custom_call" | custom-call | tf_op jit(solution)/shard_map/pallas_call | solution.py:768
  (1 shorter events, 0.0 us)
Async XLA Ops:
  0.6 12.8 %copy-start.2 = (bf16[128,1536]{1,0:T(8,128)(2,1)S(1)}, bf16[128,1536]{1,0:T(8,128)(2,1)}, u32[]{:S(2)}) copy-start(bf16[128,1536]{1,0:T(8,128)(2,1)} %tokens_ref.2) | copy-start | bytes 1179652
  0.6 12.8 %copy-start.3 = (bf16[128,1536]{1,0:T(8,128)(2,1)S(1)}, bf16[128,1536]{1,0:T(8,128)(2,1)}, u32[]{:S(2)}) copy-start(bf16[128,1536]{1,0:T(8,128)(2,1)} %cotangent_ref.2) | copy-start | bytes 1179652
  0.7 12.8 %copy-start.4 = (bf16[32,3,1536]{2,0,1:T(8,128)(2,1)S(1)}, bf16[32,3,1536]{2,0,1:T(8,128)(2,1)}, u32[]{:S(2)}) copy-start(bf16[32,3,1536]{2,0,1:T(8,128)(2,1)} %param.12) | copy-start | bytes 884740
  0.7 12.7 %copy-start.9 = (s32[32]{0:T(128)S(1)}, s32[32]{0:T(128)}, u32[]{:S(2)}) copy-start(s32[32]{0:T(128)} %counts_ref.9) | copy-start | bytes 388
  0.7 14.3 %copy-start = (bf16[1536,3,128]{2,0,1:T(8,128)(2,1)S(1)}, bf16[1536,3,128]{2,0,1:T(8,128)(2,1)}, u32[]{:S(2)}) copy-start(bf16[1536,3,128]{2,0,1:T(8,128)(2,1)} %param.9) | copy-start | bytes 3538948
  0.7 14.3 %copy-start.1 = (bf16[128,1536]{1,0:T(8,128)(2,1)S(1)}, bf16[128,1536]{1,0:T(8,128)(2,1)}, u32[]{:S(2)}) copy-start(bf16[128,1536]{1,0:T(8,128)(2,1)} %w_out_ref.2) | copy-start | bytes 1179652
  4.2 14.4 %all-to-all-start = ((bf16[4,128,256]{2,1,0:T(8,128)(2,1)}), bf16[4,128,256]{2,1,0:T(8,128)(2,1)S(1)}, u32[]{:S(2)}, u32[]{:S(2)}) async-start(bf16[4,128,256]{2,1,0:T(8,128)(2,1)} %get-tuple-element.36), calls=%async_computation | async-start | bytes 524288 | tf_op jit(solution)/shard_map/all_to_all | solution.py:795
  14.2 0.8 %copy-start.5 = (f32[4,16,1536]{2,1,0:T(8,128)}, f32[4,16,1536]{2,1,0:T(8,128)S(1)}, u32[]{:S(2)}) copy-start(f32[4,16,1536]{2,1,0:T(8,128)S(1)} %get-tuple-element.46.factors_ref) | copy-start | bytes 1179652
  15.0 0.8 %copy-start.8 = (bf16[2,64,128]{2,1,0:T(8,128)(2,1)S(1)}, bf16[2,64,128]{2,1,0:T(8,128)(2,1)}, u32[]{:S(2)}) copy-start(bf16[2,64,128]{2,1,0:T(8,128)(2,1)} %get-tuple-element.44.raw_ref) | copy-start | bytes 98308
  18.6 12.0 %collective-permute-start.2 = (bf16[512,256]{1,0:T(8,128)(2,1)S(1)}, bf16[512,256]{1,0:T(8,128)(2,1)S(1)}, u32[]{:S(2)}, u32[]{:S(2)}) collective-permute-start(bf16[512,256]{1,0:T(8,128)(2,1)S(1)} %bitcast.6), channel_id=1, source_target_pairs={{0,32},{64,96},{128,160},{192,224},{256,288},{320,352},{384,416},{... | collective-permute-start | bytes 786440 | tf_op jit(solution)/shard_map/ppermute | solution.py:801
  20.5 14.8 %collective-permute-start.1 = (bf16[512,256]{1,0:T(8,128)(2,1)S(1)}, bf16[512,256]{1,0:T(8,128)(2,1)S(1)}, u32[]{:S(2)}, u32[]{:S(2)}) collective-permute-start(bf16[512,256]{1,0:T(8,128)(2,1)S(1)} %bitcast.7), channel_id=1, source_target_pairs={{480,0},{32,64},{96,128},{160,192},{224,256},{288,320},{352,384},{... | collective-permute-start | bytes 786440 | tf_op jit(solution)/shard_map/ppermute | solution.py:801
  28.7 9.4 %collective-permute-start = (bf16[256,256]{1,0:T(8,128)(2,1)S(1)}, bf16[256,256]{1,0:T(8,128)(2,1)S(1)}, u32[]{:S(2)}, u32[]{:S(2)}) collective-permute-start(bf16[256,256]{1,0:T(8,128)(2,1)S(1)} %bitcast.11), channel_id=1, source_target_pairs={{448,0},{465,1},{80,16},{65,17},{480,32},{497,33},{112,48},{97,49}... | collective-permute-start | bytes 393224 | tf_op jit(solution)/shard_map/ppermute | solution.py:812
  31.8 15.7 %collective-permute-start.3 = (bf16[6272,128]{1,0:T(8,128)(2,1)S(1)}, bf16[6272,128]{1,0:T(8,128)(2,1)S(1)}, u32[]{:S(2)}, u32[]{:S(2)}) collective-permute-start(bf16[6272,128]{1,0:T(8,128)(2,1)S(1)} %shard_map.88.weights_ref), channel_id=1, source_target_pairs={{0,1},{1,0},{2,3},{3,2},{4,5},{5,4},{6,7},{7,6},{8,9},{9,8},{10,11... | collective-permute-start | bytes 4816904 | tf_op jit(solution)/shard_map/ppermute | solution.py:819
  38.1 9.3 %copy-start.7 = (bf16[2,64,128]{2,1,0:T(8,128)(2,1)S(1)}, bf16[2,64,128]{2,1,0:T(8,128)(2,1)}, u32[]{:S(2)}) copy-start(bf16[2,64,128]{2,1,0:T(8,128)(2,1)} %get-tuple-element.68.raw_ref) | copy-start | bytes 98308
  38.1 9.3 %copy-start.10 = (f32[2,64]{1,0:T(2,128)S(1)}, f32[2,64]{1,0:T(2,128)}, u32[]{:S(2)}) copy-start(f32[2,64]{1,0:T(2,128)} %gains_ref.3) | copy-start | bytes 1540
  47.4 13.4 %copy-start.6 = (f32[4,16,1536]{2,1,0:T(8,128)S(1)}, f32[4,16,1536]{2,1,0:T(8,128)}, u32[]{:S(2)}) copy-start(f32[4,16,1536]{2,1,0:T(8,128)} %copy-done.5) | copy-start | bytes 1179652
